TPU v7x, 512 devices: a whole 4x4x16 slice. The times are simulated.
512 devices in a mesh: wide: 128 (over x, z, core), narrow: 4 (over y).
Axes of the slice: x: 4, y: 4, z: 16, core: 2. Of those that a mesh axis runs over, the one named last changes fastest.
Arguments:
- positions: float32 [3, 1048576], P(None, ('wide', 'narrow')), as said below
- directions: float32 [3, 1048576], P(None, ('wide', 'narrow')), may hold values from -0.6 to 0.6
- radius: float32 [1048576], P(('wide', 'narrow')), may hold values from 0.01 to 0.05
- currents: float32 [16, 1048576], P(None, ('wide', 'narrow')), may hold values from -6 to 6
- pair_target: int32 [4096, 32], P(('wide', 'narrow')), may hold values from 0 to 223, as said below
- pair_count: int32 [4096], P(('wide', 'narrow')), may hold values from 1 to 32
Outputs:
- voltages: float32 [16, 1048576], P(None, ('wide', 'narrow'))
Inputs may be any that keep to these rules, and one draw needn't show every extreme that they name: The partner slab i // 32 + pair_target[i, s] // 32 exists for every slot, used or not. `positions`: the third coordinate of a filament whose block lies in slab s is between 0.1 * s and 0.1 * (s + 2).
All inputs are finite; a program needn't handle non-finite values.
Results may differ from a plain program's by a relative error of at most 0.0029.
Values sent between devices are 32-bit elements; how exact they have to be, the bound alone decides.
A program may use at most 128 MiB of HBM per device.

v0:
```python
import jax
import jax.numpy as jnp
from jax import lax
from jax.sharding import PartitionSpec as P

FIL = 256
REACH = 6
BATCH = 16


def from_behind(value, axis, steps):
    count = lax.axis_size(axis)
    initial, last = (max(0, -steps), min(count, count - steps))
    return lax.ppermute(value, axis, [(source, source + steps) for source in range(initial, last)])


def kernel_tile(pos_a, dir_a, rad_a, pos_b, dir_b, rad_b):
    gap = rad_a[..., :, None] ** 2 + rad_b[..., None, :] ** 2
    along = jnp.zeros_like(gap)
    for comp in range(3):
        diff = pos_a[comp][..., :, None] - pos_b[comp][..., None, :]
        gap = gap + diff * diff
        along = along + dir_a[comp][..., :, None] * dir_b[comp][..., None, :]
    rounded = lax.optimization_barrier((along / jnp.sqrt(gap)).astype(jnp.bfloat16))
    return rounded.astype(jnp.float32)


def pick_pairs(firsts, seconds, valid, owner, member):
    firsts = firsts.reshape(-1)
    seconds = seconds.reshape(-1)
    valid = valid.reshape(-1)
    owner = owner.reshape(-1)
    mine = valid & (owner == member)
    order = jnp.argsort(jnp.where(mine, 0, 1).astype(jnp.int32), stable=True)
    padding = jnp.zeros((BATCH,), jnp.int32)
    return (
        jnp.concatenate([firsts[order], padding]),
        jnp.concatenate([seconds[order], padding]),
        jnp.sum(mine.astype(jnp.int32)),
    )


def run_pairs(acc, picked, windows):
    firsts, seconds, count = picked
    pos_w, dir_w, rad_w, cur_w = windows
    lanes = jnp.arange(BATCH, dtype=jnp.int32)
    high = lax.Precision.HIGHEST

    def one_batch(turn, values):
        start = turn * BATCH
        first = lax.dynamic_slice_in_dim(firsts, start, BATCH, 0)
        second = lax.dynamic_slice_in_dim(seconds, start, BATCH, 0)
        live = (start + lanes < count).astype(jnp.float32)
        tiles = kernel_tile(
            jnp.take(pos_w, first, axis=1),
            jnp.take(dir_w, first, axis=1),
            jnp.take(rad_w, first, axis=0),
            jnp.take(pos_w, second, axis=1),
            jnp.take(dir_w, second, axis=1),
            jnp.take(rad_w, second, axis=0),
        )
        ahead = jnp.einsum(
            "pkb,kab->pka",
            jnp.take(cur_w, second, axis=1),
            tiles,
            precision=high,
            preferred_element_type=jnp.float32,
        )
        values = values.at[:, first].add(ahead * live[None, :, None])
        behind = jnp.einsum(
            "pka,kab->pkb",
            jnp.take(cur_w, first, axis=1),
            tiles,
            precision=high,
            preferred_element_type=jnp.float32,
        )
        values = values.at[:, second].add(behind * live[None, :, None])
        return values

    turns = (count + BATCH - 1) // BATCH
    return lax.fori_loop(0, turns, one_batch, acc)


def reach_out(unit, offsets):
    fetched = {0: unit}
    for offset in offsets:
        if offset != 0:
            fetched[offset] = from_behind(
                (unit[0], unit[1], unit[2], unit[3], unit[4], unit[5]), "wide", -offset
            )
    return fetched


def send_back(parts):
    total = parts[0]
    for offset in range(1, REACH + 1):
        total = total + from_behind(parts[offset], "wide", offset)
    return total


def narrow_sum(partial_value):
    return lax.psum_scatter(partial_value, "narrow", scatter_dimension=2, tiled=True)


def on_device(positions, directions, radius, currents, pair_target, pair_count):
    width = lax.axis_size("narrow")
    member = lax.axis_index("narrow")
    blk = pair_count.shape[0]
    maxp = pair_target.shape[1]
    span = blk * width
    ports = currents.shape[0]
    offsets = list(range(0, REACH + 1))
    own_parts = (positions, directions, radius, currents, pair_target, pair_count)
    unit = (
        lax.all_gather(own_parts[0], "narrow", axis=1, tiled=True),
        lax.all_gather(own_parts[1], "narrow", axis=1, tiled=True),
        lax.all_gather(own_parts[2], "narrow", axis=0, tiled=True),
        lax.all_gather(own_parts[3], "narrow", axis=1, tiled=True),
        lax.all_gather(own_parts[4], "narrow", axis=0, tiled=True),
        lax.all_gather(own_parts[5], "narrow", axis=0, tiled=True),
    )
    fetched = reach_out(unit, offsets)
    ordered = [fetched[offset] for offset in offsets]
    stacked = (
        jnp.stack([item[0] for item in ordered], axis=1),
        jnp.stack([item[1] for item in ordered], axis=1),
        jnp.stack([item[2] for item in ordered], axis=0),
        jnp.stack([item[3] for item in ordered], axis=1),
        jnp.stack([item[4] for item in ordered], axis=0),
        jnp.stack([item[5] for item in ordered], axis=0),
    )
    n_off = len(offsets)
    nblocks = n_off * span
    windows = (
        stacked[0].reshape(3, nblocks, FIL),
        stacked[1].reshape(3, nblocks, FIL),
        stacked[2].reshape(nblocks, FIL),
        stacked[3].reshape(ports, nblocks, FIL),
    )
    targets = stacked[4]
    counts = stacked[5]
    base = -offsets[0]
    slots = jnp.arange(maxp, dtype=jnp.int32)
    blocks_here = jnp.arange(span, dtype=jnp.int32)
    shape_pairs = (span, maxp)
    firsts = jnp.broadcast_to(base * span + blocks_here[:, None], shape_pairs)
    seconds = base * span + targets[base]
    valid = slots[None, :] < counts[base][:, None]
    owner = jnp.broadcast_to((blocks_here // blk)[:, None], shape_pairs)
    acc = jnp.zeros((ports, nblocks, FIL), jnp.float32)
    forward_pairs = pick_pairs(firsts, seconds, valid, owner, member)
    acc = run_pairs(acc, forward_pairs, windows)
    parts = [
        acc[:, offset * span : (offset + 1) * span].reshape(ports, span * FIL)
        for offset in range(REACH + 1)
    ]
    total = narrow_sum(send_back(parts).reshape(ports, 1, span * FIL))[:, 0]
    own_tiles = kernel_tile(
        positions.reshape(3, blk, FIL),
        directions.reshape(3, blk, FIL),
        radius.reshape(blk, FIL),
        positions.reshape(3, blk, FIL),
        directions.reshape(3, blk, FIL),
        radius.reshape(blk, FIL),
    )
    own_terms = jnp.einsum(
        "kab,pkb->pka",
        own_tiles,
        currents.reshape(ports, blk, FIL),
        precision=lax.Precision.HIGHEST,
        preferred_element_type=jnp.float32,
    ).reshape(ports, blk * FIL)
    return total + own_terms


def solution(mesh):
    return jax.shard_map(
        on_device,
        mesh=mesh,
        in_specs=(
            P(None, ("wide", "narrow")),
            P(None, ("wide", "narrow")),
            P(("wide", "narrow")),
            P(None, ("wide", "narrow")),
            P(("wide", "narrow"), None),
            P(("wide", "narrow")),
        ),
        out_specs=P(None, ("wide", "narrow")),
        check_vma=False,
    )
```

profile of v0, /device:TPU:2, one launch (start us, length us, event | category | flops | bytes accessed | tf_op | source)
XLA Modules:
  0.0 835.0 jit_solution(7557723468550591763)
XLA Ops:
  6.5 12.6 %all_gather.21 = f32[8192]{0:T(1024)S(1)} all-gather(f32[2048]{0:T(1024)} %param.16), channel_id=1, replica_groups=mesh['wide'=128,'narrow'=4] {'narrow'}, dimensions={0}, use_global_device_ids=true | all-gather | bytes 40960 | tf_op jit(solution)/shard_map/all_gather | solution.py:117
  19.2 12.3 %collective-permute-start.11 = (f32[8192]{0:T(1024)S(1)}, f32[8192]{0:T(1024)S(1)}, u32[]{:S(2)}, u32[]{:S(2)}) collective-permute-start(f32[8192]{0:T(1024)S(1)} %all_gather.21), channel_id=1, source_target_pairs={{24,0},{28,4},{32,8},{36,12},{40,16},{44,20},{48,24},{52,28},{56,3... | collective-permute-start | bytes 98312 | tf_op jit(solution)/shard_map/ppermute | solution.py:14
  46.8 7.8 all-reduce.2
  54.6 12.3 %all_gather.22 = f32[3,8192]{1,0:T(4,128)S(1)} all-gather(f32[3,2048]{1,0:T(4,128)} %param.14), channel_id=1, replica_groups=mesh['wide'=128,'narrow'=4] {'narrow'}, dimensions={1}, use_global_device_ids=true | all-gather | bytes 122880 | tf_op jit(solution)/shard_map/all_gather | solution.py:115
  66.9 12.4 %all_gather.19 = f32[3,8192]{1,0:T(4,128)S(1)} all-gather(f32[3,2048]{1,0:T(4,128)} %param.15), channel_id=1, replica_groups=mesh['wide'=128,'narrow'=4] {'narrow'}, dimensions={1}, use_global_device_ids=true | all-gather | bytes 122880 | tf_op jit(solution)/shard_map/all_gather | solution.py:116
  79.3 13.0 %all_gather.23 = f32[16,8192]{1,0:T(8,128)S(1)} all-gather(f32[16,2048]{1,0:T(8,128)} %param.17), channel_id=1, replica_groups=mesh['wide'=128,'narrow'=4] {'narrow'}, dimensions={1}, use_global_device_ids=true | all-gather | bytes 655360 | tf_op jit(solution)/shard_map/all_gather | solution.py:118
  103.0 12.1 %all_gather.20 = s32[32,32]{1,0:T(8,128)S(1)} all-gather(s32[8,32]{1,0:T(8,128)} %param.18), channel_id=1, replica_groups=mesh['wide'=128,'narrow'=4] {'narrow'}, dimensions={0}, use_global_device_ids=true | all-gather | bytes 5120 | tf_op jit(solution)/shard_map/all_gather | solution.py:119
  137.4 16.6 %collective-permute-done.1 = f32[3,8192]{1,0:T(4,128)S(1)} collective-permute-done((f32[3,8192]{1,0:T(4,128)S(1)}, f32[3,8192]{1,0:T(4,128)S(1)}, u32[]{:S(2)}, u32[]{:S(2)}) %collective-permute-start.1) | collective-permute-done | bytes 98336 | tf_op jit(solution)/shard_map/ppermute | solution.py:14
  170.7 12.0 %collective-permute-done.12 = f32[3,8192]{1,0:T(4,128)S(1)} collective-permute-done((f32[3,8192]{1,0:T(4,128)S(1)}, f32[3,8192]{1,0:T(4,128)S(1)}, u32[]{:S(2)}, u32[]{:S(2)}) %collective-permute-start.12) | collective-permute-done | bytes 98336 | tf_op jit(solution)/shard_map/ppermute | solution.py:14
  184.7 5.6 collective-permute-done.13
  190.3 4.7 collective-permute-start.23
  205.3 95.8 %collective-permute-done.18 = f32[16,8192]{1,0:T(8,128)S(1)} collective-permute-done((f32[16,8192]{1,0:T(8,128)S(1)}, f32[16,8192]{1,0:T(8,128)S(1)}, u32[]{:S(2)}, u32[]{:S(2)}) %collective-permute-start.18) | collective-permute-done | bytes 524320 | tf_op jit(solution)/shard_map/ppermute | solution.py:14
  303.8 11.4 %collective-permute-done.19 = f32[16,8192]{1,0:T(8,128)S(1)} collective-permute-done((f32[16,8192]{1,0:T(8,128)S(1)}, f32[16,8192]{1,0:T(8,128)S(1)}, u32[]{:S(2)}, u32[]{:S(2)}) %collective-permute-start.19) | collective-permute-done | bytes 524320 | tf_op jit(solution)/shard_map/ppermute | solution.py:14
  319.4 6.1 copy.42
  325.6 5.7 reshape.159
  331.3 6.0 copy.43
  339.5 340.0 %while.11 = (s32[]{:T(128)}, f32[16,224,256]{2,0,1:T(8,128)}, s32[]{:T(128)}, s32[1040]{0:T(1024)S(1)}, f32[3,224,256]{2,0,1:T(4,128)S(1)}, /*index=5*/s32[1040]...) while((s32[]{:T(128)}, f32[16,224,256]{2,0,1:T(8,128)}, ...), condition=%wide.region_5.9_spmd.clone, body=%wide.region_2.8_spmd.clone.sunk | while | flops 420940032 | bytes 11904511 | solution.py:81
  686.3 12.2 %collective-permute-start.26 = (f32[16,8192]{1,0:T(8,128)S(1)}, f32[16,8192]{1,0:T(8,128)S(1)}, u32[]{:S(2)}, u32[]{:S(2)}) collective-permute-start(f32[16,8192]{1,0:T(8,128)S(1)} %bitcast.200), channel_id=1, source_target_pairs={{0,12},{4,16},{8,20},{12,24},{16,28},{20,32},{24,36},{28,40},{32,4... | collective-permute-start | bytes 1572872 | tf_op jit(solution)/shard_map/ppermute | solution.py:14
  704.7 8.4 %collective-permute-done.25 = f32[16,8192]{1,0:T(8,128)S(1)} collective-permute-done((f32[16,8192]{1,0:T(8,128)S(1)}, f32[16,8192]{1,0:T(8,128)S(1)}, u32[]{:S(2)}, u32[]{:S(2)}) %collective-permute-start.25) | collective-permute-done | bytes 524320 | tf_op jit(solution)/shard_map/ppermute | solution.py:14
  713.1 29.6 %collective-permute-done.26 = f32[16,8192]{1,0:T(8,128)S(1)} collective-permute-done((f32[16,8192]{1,0:T(8,128)S(1)}, f32[16,8192]{1,0:T(8,128)S(1)}, u32[]{:S(2)}, u32[]{:S(2)}) %collective-permute-start.26) | collective-permute-done | bytes 524320 | tf_op jit(solution)/shard_map/ppermute | solution.py:14
  742.7 7.8 collective-permute-done.27
  750.5 24.3 %collective-permute-done.28 = f32[16,8192]{1,0:T(8,128)S(1)} collective-permute-done((f32[16,8192]{1,0:T(8,128)S(1)}, f32[16,8192]{1,0:T(8,128)S(1)}, u32[]{:S(2)}, u32[]{:S(2)}) %collective-permute-start.28) | collective-permute-done | bytes 524320 | tf_op jit(solution)/shard_map/ppermute | solution.py:14
  774.9 12.0 %collective-permute-done.24 = f32[16,8192]{1,0:T(8,128)S(1)} collective-permute-done((f32[16,8192]{1,0:T(8,128)S(1)}, f32[16,8192]{1,0:T(8,128)S(1)}, u32[]{:S(2)}, u32[]{:S(2)}) %collective-permute-start.24) | collective-permute-done | bytes 524320 | tf_op jit(solution)/shard_map/ppermute | solution.py:14
  791.3 35.2 %reduce-scatter.2.cloned.1.call-done = f32[16,1,2048]{2,0,1:T(8,128)} async-done(((f32[16,1,8192]{2,0,1:T(8,128)}), f32[16,1,2048]{2,0,1:T(8,128)}) %reduce-scatter.2.cloned.1.call-update) | async-done | bytes 131088 | tf_op jit(solution)/shard_map/reduce_scatter | solution.py:102
  (675 shorter events, 440.4 us)
Async XLA Ops:
  6.5 820.0 %reduce-scatter.2.cloned.1.call-start = ((), (), s32[]{:S(2)}) async-start(), calls=%async_computation.1 | async-start | bytes 655360 | tf_op jit(solution)/shard_map/reduce_scatter | solution.py:102
  19.2 79.2 %collective-permute-start.11 = (f32[8192]{0:T(1024)S(1)}, f32[8192]{0:T(1024)S(1)}, u32[]{:S(2)}, u32[]{:S(2)}) collective-permute-start(f32[8192]{0:T(1024)S(1)} %all_gather.21), channel_id=1, source_target_pairs={{24,0},{28,4},{32,8},{36,12},{40,16},{44,20},{48,24},{52,28},{56,3... | collective-permute-start | bytes 98312 | tf_op jit(solution)/shard_map/ppermute | solution.py:14
  31.4 68.9 %collective-permute-start.10 = (f32[8192]{0:T(1024)S(1)}, f32[8192]{0:T(1024)S(1)}, u32[]{:S(2)}, u32[]{:S(2)}) collective-permute-start(f32[8192]{0:T(1024)S(1)} %all_gather.21), channel_id=1, source_target_pairs={{20,0},{24,4},{28,8},{32,12},{36,16},{40,20},{44,24},{48,28},{52,3... | collective-permute-start | bytes 98312 | tf_op jit(solution)/shard_map/ppermute | solution.py:14
  33.4 91.0 %collective-permute-start.9 = (f32[8192]{0:T(1024)S(1)}, f32[8192]{0:T(1024)S(1)}, u32[]{:S(2)}, u32[]{:S(2)}) collective-permute-start(f32[8192]{0:T(1024)S(1)} %all_gather.21), channel_id=1, source_target_pairs={{16,0},{20,4},{24,8},{28,12},{32,16},{36,20},{40,24},{44,28},{48,3... | collective-permute-start | bytes 98312 | tf_op jit(solution)/shard_map/ppermute | solution.py:14
  37.9 88.4 %collective-permute-start.8 = (f32[8192]{0:T(1024)S(1)}, f32[8192]{0:T(1024)S(1)}, u32[]{:S(2)}, u32[]{:S(2)}) collective-permute-start(f32[8192]{0:T(1024)S(1)} %all_gather.21), channel_id=1, source_target_pairs={{12,0},{16,4},{20,8},{24,12},{28,16},{32,20},{36,24},{40,28},{44,3... | collective-permute-start | bytes 98312 | tf_op jit(solution)/shard_map/ppermute | solution.py:14
  41.3 87.0 %collective-permute-start.7 = (f32[8192]{0:T(1024)S(1)}, f32[8192]{0:T(1024)S(1)}, u32[]{:S(2)}, u32[]{:S(2)}) collective-permute-start(f32[8192]{0:T(1024)S(1)} %all_gather.21), channel_id=1, source_target_pairs={{8,0},{12,4},{16,8},{20,12},{24,16},{28,20},{32,24},{36,28},{40,32... | collective-permute-start | bytes 98312 | tf_op jit(solution)/shard_map/ppermute | solution.py:14
  98.4 34.3 %collective-permute-start.6 = (f32[8192]{0:T(1024)S(1)}, f32[8192]{0:T(1024)S(1)}, u32[]{:S(2)}, u32[]{:S(2)}) collective-permute-start(f32[8192]{0:T(1024)S(1)} %all_gather.21), channel_id=1, source_target_pairs={{4,0},{8,4},{12,8},{16,12},{20,16},{24,20},{28,24},{32,28},{36,32}... | collective-permute-start | bytes 98312 | tf_op jit(solution)/shard_map/ppermute | solution.py:14
  100.3 34.8 %collective-permute-start = (f32[3,8192]{1,0:T(4,128)S(1)}, f32[3,8192]{1,0:T(4,128)S(1)}, u32[]{:S(2)}, u32[]{:S(2)}) collective-permute-start(f32[3,8192]{1,0:T(4,128)S(1)} %all_gather.19), channel_id=1, source_target_pairs={{4,0},{8,4},{12,8},{16,12},{20,16},{24,20},{28,24},{32,28},{36,32}... | collective-permute-start | bytes 294920 | tf_op jit(solution)/shard_map/ppermute | solution.py:14
  124.4 44.1 %collective-permute-start.5 = (f32[3,8192]{1,0:T(4,128)S(1)}, f32[3,8192]{1,0:T(4,128)S(1)}, u32[]{:S(2)}, u32[]{:S(2)}) collective-permute-start(f32[3,8192]{1,0:T(4,128)S(1)} %all_gather.19), channel_id=1, source_target_pairs={{24,0},{28,4},{32,8},{36,12},{40,16},{44,20},{48,24},{52,28},{56,3... | collective-permute-start | bytes 294920 | tf_op jit(solution)/shard_map/ppermute | solution.py:14
  126.4 39.2 %collective-permute-start.4 = (f32[3,8192]{1,0:T(4,128)S(1)}, f32[3,8192]{1,0:T(4,128)}, u32[]{:S(2)}, u32[]{:S(2)}) collective-permute-start(f32[3,8192]{1,0:T(4,128)S(1)} %all_gather.19), channel_id=1, source_target_pairs={{20,0},{24,4},{28,8},{32,12},{36,16},{40,20},{44,24},{48,28},{52,3... | collective-permute-start | bytes 294920 | tf_op jit(solution)/shard_map/ppermute | solution.py:14
  128.3 33.3 %collective-permute-start.3 = (f32[3,8192]{1,0:T(4,128)S(1)}, f32[3,8192]{1,0:T(4,128)}, u32[]{:S(2)}, u32[]{:S(2)}) collective-permute-start(f32[3,8192]{1,0:T(4,128)S(1)} %all_gather.19), channel_id=1, source_target_pairs={{16,0},{20,4},{24,8},{28,12},{32,16},{36,20},{40,24},{44,28},{48,3... | collective-permute-start | bytes 294920 | tf_op jit(solution)/shard_map/ppermute | solution.py:14
  154.0 49.2 %collective-permute-start.17 = (f32[3,8192]{1,0:T(4,128)S(1)}, f32[3,8192]{1,0:T(4,128)S(1)}, u32[]{:S(2)}, u32[]{:S(2)}) collective-permute-start(f32[3,8192]{1,0:T(4,128)S(1)} %all_gather.22), channel_id=1, source_target_pairs={{24,0},{28,4},{32,8},{36,12},{40,16},{44,20},{48,24},{52,28},{56,3... | collective-permute-start | bytes 294920 | tf_op jit(solution)/shard_map/ppermute | solution.py:14
  156.0 45.1 %collective-permute-start.16 = (f32[3,8192]{1,0:T(4,128)S(1)}, f32[3,8192]{1,0:T(4,128)S(1)}, u32[]{:S(2)}, u32[]{:S(2)}) collective-permute-start(f32[3,8192]{1,0:T(4,128)S(1)} %all_gather.22), channel_id=1, source_target_pairs={{20,0},{24,4},{28,8},{32,12},{36,16},{40,20},{44,24},{48,28},{52,3... | collective-permute-start | bytes 294920 | tf_op jit(solution)/shard_map/ppermute | solution.py:14
  161.6 36.2 %collective-permute-start.15 = (f32[3,8192]{1,0:T(4,128)S(1)}, f32[3,8192]{1,0:T(4,128)S(1)}, u32[]{:S(2)}, u32[]{:S(2)}) collective-permute-start(f32[3,8192]{1,0:T(4,128)S(1)} %all_gather.22), channel_id=1, source_target_pairs={{16,0},{20,4},{24,8},{28,12},{32,16},{36,20},{40,24},{44,28},{48,3... | collective-permute-start | bytes 294920 | tf_op jit(solution)/shard_map/ppermute | solution.py:14
  165.6 29.4 %collective-permute-start.14 = (f32[3,8192]{1,0:T(4,128)S(1)}, f32[3,8192]{1,0:T(4,128)S(1)}, u32[]{:S(2)}, u32[]{:S(2)}) collective-permute-start(f32[3,8192]{1,0:T(4,128)S(1)} %all_gather.22), channel_id=1, source_target_pairs={{12,0},{16,4},{20,8},{24,12},{28,16},{32,20},{36,24},{40,28},{44,3... | collective-permute-start | bytes 294920 | tf_op jit(solution)/shard_map/ppermute | solution.py:14
  190.3 128.4 %collective-permute-start.23 = (f32[16,8192]{1,0:T(8,128)S(1)}, f32[16,8192]{1,0:T(8,128)S(1)}, u32[]{:S(2)}, u32[]{:S(2)}) collective-permute-start(f32[16,8192]{1,0:T(8,128)S(1)} %all_gather.23), channel_id=1, source_target_pairs={{24,0},{28,4},{32,8},{36,12},{40,16},{44,20},{48,24},{52,28},{56,3... | collective-permute-start | bytes 1572872 | tf_op jit(solution)/shard_map/ppermute | solution.py:14
  195.0 122.8 %collective-permute-start.22 = (f32[16,8192]{1,0:T(8,128)S(1)}, f32[16,8192]{1,0:T(8,128)S(1)}, u32[]{:S(2)}, u32[]{:S(2)}) collective-permute-start(f32[16,8192]{1,0:T(8,128)S(1)} %all_gather.23), channel_id=1, source_target_pairs={{20,0},{24,4},{28,8},{32,12},{36,16},{40,20},{44,24},{48,28},{52,3... | collective-permute-start | bytes 1572872 | tf_op jit(solution)/shard_map/ppermute | solution.py:14
  197.8 119.1 %collective-permute-start.21 = (f32[16,8192]{1,0:T(8,128)S(1)}, f32[16,8192]{1,0:T(8,128)S(1)}, u32[]{:S(2)}, u32[]{:S(2)}) collective-permute-start(f32[16,8192]{1,0:T(8,128)S(1)} %all_gather.23), channel_id=1, source_target_pairs={{16,0},{20,4},{24,8},{28,12},{32,16},{36,20},{40,24},{44,28},{48,3... | collective-permute-start | bytes 1572872 | tf_op jit(solution)/shard_map/ppermute | solution.py:14
  201.0 115.1 %collective-permute-start.20 = (f32[16,8192]{1,0:T(8,128)S(1)}, f32[16,8192]{1,0:T(8,128)S(1)}, u32[]{:S(2)}, u32[]{:S(2)}) collective-permute-start(f32[16,8192]{1,0:T(8,128)S(1)} %all_gather.23), channel_id=1, source_target_pairs={{12,0},{16,4},{20,8},{24,12},{28,16},{32,20},{36,24},{40,28},{44,3... | collective-permute-start | bytes 1572872 | tf_op jit(solution)/shard_map/ppermute | solution.py:14
  203.2 97.8 %collective-permute-start.18 = (f32[16,8192]{1,0:T(8,128)S(1)}, f32[16,8192]{1,0:T(8,128)S(1)}, u32[]{:S(2)}, u32[]{:S(2)}) collective-permute-start(f32[16,8192]{1,0:T(8,128)S(1)} %all_gather.23), channel_id=1, source_target_pairs={{4,0},{8,4},{12,8},{16,12},{20,16},{24,20},{28,24},{32,28},{36,32}... | collective-permute-start | bytes 1572872 | tf_op jit(solution)/shard_map/ppermute | solution.py:14
  686.3 56.4 %collective-permute-start.26 = (f32[16,8192]{1,0:T(8,128)S(1)}, f32[16,8192]{1,0:T(8,128)S(1)}, u32[]{:S(2)}, u32[]{:S(2)}) collective-permute-start(f32[16,8192]{1,0:T(8,128)S(1)} %bitcast.200), channel_id=1, source_target_pairs={{0,12},{4,16},{8,20},{12,24},{16,28},{20,32},{24,36},{28,40},{32,4... | collective-permute-start | bytes 1572872 | tf_op jit(solution)/shard_map/ppermute | solution.py:14
  698.5 52.0 %collective-permute-start.27 = (f32[16,8192]{1,0:T(8,128)S(1)}, f32[16,8192]{1,0:T(8,128)S(1)}, u32[]{:S(2)}, u32[]{:S(2)}) collective-permute-start(f32[16,8192]{1,0:T(8,128)S(1)} %bitcast.199), channel_id=1, source_target_pairs={{0,16},{4,20},{8,24},{12,28},{16,32},{20,36},{24,40},{28,44},{32,4... | collective-permute-start | bytes 1572872 | tf_op jit(solution)/shard_map/ppermute | solution.py:14
  700.4 74.5 %collective-permute-start.28 = (f32[16,8192]{1,0:T(8,128)S(1)}, f32[16,8192]{1,0:T(8,128)S(1)}, u32[]{:S(2)}, u32[]{:S(2)}) collective-permute-start(f32[16,8192]{1,0:T(8,128)S(1)} %bitcast.198), channel_id=1, source_target_pairs={{0,20},{4,24},{8,28},{12,32},{16,36},{20,40},{24,44},{28,48},{32,5... | collective-permute-start | bytes 1572872 | tf_op jit(solution)/shard_map/ppermute | solution.py:14
  702.4 84.5 %collective-permute-start.24 = (f32[16,8192]{1,0:T(8,128)S(1)}, f32[16,8192]{1,0:T(8,128)S(1)}, u32[]{:S(2)}, u32[]{:S(2)}) collective-permute-start(f32[16,8192]{1,0:T(8,128)S(1)} %bitcast.197), channel_id=1, source_target_pairs={{0,4},{4,8},{8,12},{12,16},{16,20},{20,24},{24,28},{28,32},{32,36}... | collective-permute-start | bytes 1572872 | tf_op jit(solution)/shard_map/ppermute | solution.py:14
  (11 other events, 544.9 us)
Sparse Core Ops, SparseCore 0:
  788.0 38.5 reduce-scatter.1
where the time goes:
time: 838 us; the launch traced here: 835 us
  waiting for transfers between devices  259 us (31%)
  local copies, waits for them, and re-layouts  177 us (21%)
  other arithmetic  172 us (21%)
  starting transfers between devices  95.7 us (11%)
  blocking collectives  70.2 us (8%)
  matrix products  42 us (5%)
  between operations  15.5 us (2%)
    ppermute x30, waiting for transfers between devices, from_behind(): lax.ppermute(value, axis, [(source, source + steps) for source in range(i...  224 us
    ppermute x30, starting transfers between devices, from_behind(): lax.ppermute(value, axis, [(source, source + steps) for source in range(i...  95.7 us
    convert_element_type x16, other arithmetic, kernel_tile(): (along / jnp.sqrt(gap)).astype(jnp.bfloat16)  69.7 us
    scatter-add x15, other arithmetic, one_batch(): values = values.at[:, first].add(ahead * live[None, :, None])  41.5 us
    gather x15, local copies, waits for them, and re-layouts, one_batch(): jnp.take(cur_w, first, axis=1)  39 us
    gather x15, local copies, waits for them, and re-layouts, one_batch(): jnp.take(cur_w, second, axis=1)  39 us
    scatter-add x15, other arithmetic, one_batch(): values = values.at[:, second].add(behind * live[None, :, None])  36.4 us
    reduce_scatter x1, waiting for transfers between devices, narrow_sum(): lax.psum_scatter(partial_value, 'narrow', scatter_dimension=2, tiled=True)  35.2 us
  transfers between devices with their start and end apart: 31, of which 11 were waited for; matrix products, arithmetic and copies ran while one was open for 3% of the time, Pallas kernels for 0%

commit v1 on v0

v1 whole, which is shorter than its diff:
```python
import functools

import jax
import jax.numpy as jnp
from jax import lax
from jax.experimental import pallas as pl
from jax.experimental.pallas import tpu as pltpu
from jax.sharding import PartitionSpec as P

FIL = 256
PORTS = 16
BLK = 8
MAXP = 32
SLAB = 32
MEMBERS = 4
HOPS = 4
ROWS = 24
WINDOW = 2 * HOPS * BLK
LIST = 40 * 32
UNROLL = 8
PARTS = 2
f32 = jnp.float32
bf16 = jnp.bfloat16
MESH = pl.DeviceIdType.MESH


def place():
    wide = lax.axis_index("wide")
    member = lax.axis_index("narrow")
    count = lax.axis_size("wide")
    core = lax.rem(wide, 2)
    twin = wide + 1 - 2 * core
    ahead = lax.rem(wide + 2, count)
    behind = lax.rem(wide + count - 2, count)
    return wide, member, core, twin, ahead, behind


def greet(devices):
    barrier = pltpu.get_barrier_semaphore()
    for device in devices:
        pl.semaphore_signal(barrier, inc=1, device_id=device, device_id_type=MESH)
    pl.semaphore_wait(barrier, len(devices))


def remote(src, dst, send, recv, device):
    return pltpu.make_async_remote_copy(
        src_ref=src, dst_ref=dst, send_sem=send, recv_sem=recv, device_id=device, device_id_type=MESH
    )


def list_pairs(rows, member, core, li_ref, lj_ref):
    lane = lax.broadcasted_iota(jnp.int32, (8, FIL), 1)
    row = lax.broadcasted_iota(jnp.int32, (8, FIL), 0)
    mine = (rows >= 0) & ((rows & 31) // BLK == member)
    hit = mine.astype(bf16)
    upper = (
        lax.broadcasted_iota(jnp.int32, (FIL, FIL), 0) <= lax.broadcasted_iota(jnp.int32, (FIL, FIL), 1)
    ).astype(bf16)
    inclusive = jnp.dot(hit, upper, preferred_element_type=f32).astype(jnp.int32)
    totals = jnp.sum(mine.astype(jnp.int32), axis=1, keepdims=True)
    base = jnp.full((8, 1), BLK, jnp.int32)
    which = lax.broadcasted_iota(jnp.int32, (8, 1), 0)
    for m in range(MEMBERS - 1):
        base = base + jnp.where(which > m, totals[m : m + 1], 0)
    spot = jnp.where(mine, base + inclusive - 1, -1)
    source = row * BLK + lane // MAXP
    partner = (core + rows // SLAB) * BLK + (rows & 7)
    high = jnp.where(mine, spot // 32, -1)
    low = jnp.where(mine, spot & 31, -1)
    out_i = jnp.zeros((40, 32), f32)
    out_j = jnp.zeros((40, 32), f32)
    spots_high = lax.broadcasted_iota(jnp.int32, (40, FIL), 0)
    spots_low = lax.broadcasted_iota(jnp.int32, (32, FIL), 0)
    contract = (((1,), (1,)), ((), ()))
    for m in range(MEMBERS):
        pick_high = spots_high == high[m : m + 1]
        pick_low = (spots_low == low[m : m + 1]).astype(f32).astype(bf16)
        put_i = jnp.where(pick_high, source[m : m + 1].astype(f32), 0.0).astype(bf16)
        put_j = jnp.where(pick_high, partner[m : m + 1].astype(f32), 0.0).astype(bf16)
        out_i = out_i + lax.dot_general(put_i, pick_low, contract, preferred_element_type=f32)
        out_j = out_j + lax.dot_general(put_j, pick_low, contract, preferred_element_type=f32)
    total = BLK + jnp.sum(totals[0:MEMBERS], axis=0, keepdims=True)
    flat = 32 * lax.broadcasted_iota(jnp.int32, (40, 32), 0) + lax.broadcasted_iota(jnp.int32, (40, 32), 1)
    diagonal = flat < BLK
    used = flat < total
    li = jnp.where(diagonal, member * BLK + flat, jnp.where(used, out_i.astype(jnp.int32), SLAB))
    lj = jnp.where(diagonal, 2 * WINDOW + core * BLK + flat, jnp.where(used, out_j.astype(jnp.int32), WINDOW))
    li_ref[...] = li
    lj_ref[...] = lj
    return total


def fetch_kernel(
    pos, dirs, rad, cur, pairs, src, par, li_ref, lj_ref, n_ref,
    own, lists, y_send, y_recv, l_send, l_recv, z_send, z_recv, c_send, c_recv, home_sem,
):
    wide, member, core, twin, ahead, behind = place()
    mates = [lax.rem(member + step, MEMBERS) for step in range(1, MEMBERS)]
    lists[...] = jnp.full((8, FIL), -1, jnp.int32)
    lists[pl.ds(member, 1)] = pairs[...]
    greet([(wide, mate) for mate in mates] + [(ahead, member), (twin, member)])
    for b in range(BLK):
        cut = slice(b * FIL, (b + 1) * FIL)
        own[b, 0:3] = pos[:, cut]
        own[b, 3:6] = dirs[:, cut]
        own[b, 6:7] = rad[:, cut]
        own[b, 7:8] = rad[:, cut]
        own[b, 8:ROWS] = cur[:, cut]
    half = BLK // PARTS

    def seat(hop, part):
        return pl.ds((2 * hop + core) * BLK + part * half, half)

    sends = []
    first = []
    for part in range(PARTS):
        copy = remote(
            own.at[pl.ds(part * half, half)], par.at[seat(1, part)], z_send.at[0, part], z_recv.at[0, part], (behind, member)
        )
        copy.start()
        first.append(copy)
    hops = [first]
    list_copies = []
    for step, mate in enumerate(mates):
        copy = remote(
            pairs, lists.at[pl.ds(member, 1)], l_send.at[step], l_recv.at[step], (wide, mate)
        )
        copy.start()
        list_copies.append(copy)
    unit_copies = []
    for step, mate in enumerate(mates):
        copy = remote(own, src.at[pl.ds(member * BLK, BLK)], y_send.at[step], y_recv.at[step], (wide, mate))
        copy.start()
        unit_copies.append(copy)
    core_copies = []
    copy = remote(own, par.at[pl.ds(core * BLK, BLK)], c_send.at[0, 0], c_recv.at[0, 0], (twin, member))
    copy.start()
    core_copies.append(copy)
    home = [
        pltpu.make_async_copy(own, src.at[pl.ds(member * BLK, BLK)], home_sem.at[0]),
        pltpu.make_async_copy(own, par.at[pl.ds(core * BLK, BLK)], home_sem.at[1]),
    ]
    for copy in home:
        copy.start()
    for copy in list_copies:
        copy.wait()
    total = list_pairs(lists[...], member, core, li_ref, lj_ref)
    n_ref[...] = jnp.broadcast_to(total, (8, 128))
    for hop in range(1, HOPS):
        later = []
        for part in range(PARTS):
            hops[hop - 1][part].wait_recv()
            if hop < HOPS - 1:
                copy = remote(
                    par.at[seat(hop, part)], par.at[seat(hop + 1, part)], z_send.at[hop, part], z_recv.at[hop, part], (behind, member)
                )
                copy.start()
                later.append(copy)
            copy = remote(
                par.at[seat(hop, part)], par.at[seat(hop, part)], c_send.at[hop, part], c_recv.at[hop, part], (twin, member)
            )
            copy.start()
            core_copies.append(copy)
        hops.append(later)
    for group in hops:
        for copy in group:
            copy.wait_send()
    for copy in unit_copies + core_copies + home:
        copy.wait()


def fetch(pos, dirs, rad, cur, pairs):
    vm = pl.BlockSpec(memory_space=pltpu.VMEM)
    hbm = pl.BlockSpec(memory_space=pl.ANY)
    dma = pltpu.SemaphoreType.DMA
    return pl.pallas_call(
        fetch_kernel,
        out_shape=[
            jax.ShapeDtypeStruct((SLAB, ROWS, FIL), f32),
            jax.ShapeDtypeStruct((WINDOW, ROWS, FIL), f32),
            jax.ShapeDtypeStruct((40, 32), jnp.int32),
            jax.ShapeDtypeStruct((40, 32), jnp.int32),
            jax.ShapeDtypeStruct((8, 128), jnp.int32),
        ],
        in_specs=[vm] * 5,
        out_specs=[hbm, hbm, vm, vm, vm],
        scratch_shapes=[
            pltpu.VMEM((BLK, ROWS, FIL), f32),
            pltpu.VMEM((8, FIL), jnp.int32),
            dma((3,)), dma((3,)), dma((3,)), dma((3,)),
            dma((3, PARTS)), dma((3, PARTS)),
            dma((HOPS, PARTS)), dma((HOPS, PARTS)),
            dma((2,)),
        ],
        compiler_params=pltpu.CompilerParams(
            collective_id=0, has_side_effects=True, vmem_limit_bytes=32 * 2**20
        ),
    )(pos, dirs, rad, cur, pairs)


def directed(block):
    cur = block[8:ROWS]
    parts = jnp.concatenate([block[3 + comp : 4 + comp] * cur for comp in range(3)], axis=0)
    head = parts.astype(bf16)
    tail = (parts - head.astype(f32)).astype(bf16)
    return jnp.concatenate([head, tail], axis=0)


def tiles_kernel(n_ref, li_ref, lj_ref, src, par, s_out, p_out, c_src, c_par, cols, even, odd):
    n = n_ref[0, 0]

    @pl.loop(0, SLAB)
    def _(i):
        block = src[i]
        c_src[i] = directed(block)
        s_out[i] = jnp.zeros((PORTS, FIL), f32)
        turned = block[0:8].T
        for place_of, row in enumerate((0, 1, 2, 6)):
            column = turned[:, row : row + 1]
            if row == 6:
                column = column * column
            cols[i, place_of] = jnp.broadcast_to(column, (FIL, 128))

    @pl.loop(0, WINDOW)
    def _(j):
        c_par[j] = directed(par[j])
        p_out[j] = jnp.zeros((PORTS, FIL), f32)

    s_out[SLAB] = jnp.zeros((PORTS, FIL), f32)
    p_out[WINDOW] = jnp.zeros((PORTS, FIL), f32)

    def pair(k):
        row, col = k // 32, k & 31
        i, j = li_ref[row, col], lj_ref[row, col]
        return i, jnp.minimum(i, SLAB - 1), jnp.minimum(j, WINDOW), j & (WINDOW - 1)

    def chunks(k, buf):
        _, i, _, j = pair(k)
        geometry = par[j, 0:8, :]

        def chunk(h, r):
            cut = slice(h * 128, h * 128 + 128)
            xb, yb, zb, rb = [jnp.broadcast_to(geometry[q : q + 1, cut], (16, 128)) for q in (0, 1, 2, 6)]
            xa, ya, za, ra = [cols[i, q, r : r + 16, :] for q in range(4)]
            dx, dy, dz = xa - xb, ya - yb, za - zb
            gap = (ra + rb * rb) + dx * dx + dy * dy + dz * dz
            buf[r : r + 16, cut] = lax.rsqrt(gap).astype(bf16)

        return [functools.partial(chunk, h, r) for h in range(2) for r in range(0, FIL, 16)]

    def fold(product, dirs):
        both = product[0 : 3 * PORTS] + product[3 * PORTS : 6 * PORTS]
        return (
            both[0:PORTS] * dirs[0:1] + both[PORTS : 2 * PORTS] * dirs[1:2]
        ) + both[2 * PORTS : 3 * PORTS] * dirs[2:3]

    def step(k_next, buf_next, k, buf):
        work = chunks(k_next, buf_next)
        i_put, i, j_put, j = pair(k)
        behind = lax.dot_general(c_src[i], buf[...], (((1,), (0,)), ((), ())), preferred_element_type=f32)
        for piece in work[:16]:
            piece()
        p_out[j_put] += fold(behind, par[j, 3:6, :])
        ahead = lax.dot_general(c_par[j], buf[...], (((1,), (1,)), ((), ())), preferred_element_type=f32)
        for piece in work[16:]:
            piece()
        s_out[i_put] += fold(ahead, src[i, 3:6, :])

    for piece in chunks(0, even):
        piece()

    @pl.loop(0, (n + UNROLL - 1) // UNROLL)
    def _(turn):
        k = UNROLL * turn
        for q in range(UNROLL):
            now, later = (even, odd) if q % 2 == 0 else (odd, even)
            step(k + q + 1, later, k + q, now)


def tiles(n, li, lj, src, par):
    sm = pl.BlockSpec(memory_space=pltpu.SMEM)
    vm = pl.BlockSpec(memory_space=pltpu.VMEM)
    return pl.pallas_call(
        tiles_kernel,
        out_shape=[
            jax.ShapeDtypeStruct((SLAB + 1, PORTS, FIL), f32),
            jax.ShapeDtypeStruct((WINDOW + 1, PORTS, FIL), f32),
        ],
        in_specs=[sm, sm, sm, vm, vm],
        out_specs=[vm, vm],
        scratch_shapes=[
            pltpu.VMEM((SLAB, 6 * PORTS, FIL), bf16),
            pltpu.VMEM((WINDOW, 6 * PORTS, FIL), bf16),
            pltpu.VMEM((SLAB, 4, FIL, 128), f32),
            pltpu.VMEM((FIL, FIL), bf16),
            pltpu.VMEM((FIL, FIL), bf16),
        ],
        compiler_params=pltpu.CompilerParams(vmem_limit_bytes=56 * 2**20),
    )(n, li, lj, src, par)


def return_kernel(
    s_part, p_part, out, x_buf, y_buf, z_buf, z_out, y_send, y_recv, z_send, z_recv, c_send, c_recv
):
    wide, member, core, twin, ahead, behind = place()
    mates = [lax.rem(member + step, MEMBERS) for step in range(1, MEMBERS)]
    greet([(wide, mate) for mate in mates] + [(behind, member), (twin, member)])
    half = BLK // PARTS
    core_copies = {}
    for hop in range(HOPS - 1, -1, -1):
        for part in range(PARTS):
            copy = remote(
                p_part.at[pl.ds((2 * hop + 1 - core) * BLK + part * half, half)],
                x_buf.at[hop, pl.ds(part * half, half)],
                c_send.at[hop, part], c_recv.at[hop, part], (twin, member),
            )
            copy.start()
            core_copies[hop, part] = copy
    unit_copies = []
    for step, mate in enumerate(mates):
        copy = remote(
            s_part.at[pl.ds(mate * BLK, BLK)], y_buf.at[step], y_send.at[step], y_recv.at[step], (wide, mate)
        )
        copy.start()
        unit_copies.append(copy)
    hops = {}
    for hop in range(HOPS - 1, -1, -1):
        for part in range(PARTS):
            cut = pl.ds(part * half, half)
            core_copies[hop, part].wait_recv()
            value = p_part[pl.ds((2 * hop + core) * BLK + part * half, half)] + x_buf[hop, cut]
            if hop < HOPS - 1:
                hops[hop + 1, part].wait_recv()
                value = value + z_buf[hop, cut]
            if hop > 0:
                z_out[hop - 1, cut] = value
                copy = remote(
                    z_out.at[hop - 1, cut], z_buf.at[hop - 1, cut],
                    z_send.at[hop - 1, part], z_recv.at[hop - 1, part], (ahead, member),
                )
                copy.start()
                hops[hop, part] = copy
            else:
                if part == 0:
                    for copy in unit_copies:
                        copy.wait_recv()
                value = value + s_part[pl.ds(member * BLK + part * half, half)]
                for step in range(MEMBERS - 1):
                    value = value + y_buf[step, cut]
                for b in range(half):
                    at = (part * half + b) * FIL
                    out[:, at : at + FIL] = value[b]
    for copy in list(core_copies.values()) + unit_copies + list(hops.values()):
        copy.wait_send()


def send_home(s_part, p_part):
    vm = pl.BlockSpec(memory_space=pltpu.VMEM)
    dma = pltpu.SemaphoreType.DMA
    return pl.pallas_call(
        return_kernel,
        out_shape=jax.ShapeDtypeStruct((PORTS, BLK * FIL), f32),
        in_specs=[vm, vm],
        out_specs=vm,
        scratch_shapes=[
            pltpu.VMEM((HOPS, BLK, PORTS, FIL), f32),
            pltpu.VMEM((MEMBERS - 1, BLK, PORTS, FIL), f32),
            pltpu.VMEM((HOPS - 1, BLK, PORTS, FIL), f32),
            pltpu.VMEM((HOPS - 1, BLK, PORTS, FIL), f32),
            dma((3,)), dma((3,)),
            dma((HOPS - 1, PARTS)), dma((HOPS - 1, PARTS)),
            dma((HOPS, PARTS)), dma((HOPS, PARTS)),
        ],
        compiler_params=pltpu.CompilerParams(
            collective_id=1, has_side_effects=True, vmem_limit_bytes=32 * 2**20
        ),
    )(s_part, p_part)


def on_device(positions, directions, radius, currents, pair_target, pair_count):
    slots = jnp.arange(MAXP, dtype=jnp.int32)
    pairs = jnp.where(slots[None, :] < pair_count[:, None], pair_target, -1).reshape(1, BLK * MAXP)
    src, par, li, lj, n = fetch(positions, directions, radius.reshape(1, BLK * FIL), currents, pairs)
    s_part, p_part = tiles(n, li, lj, src, par)
    return send_home(s_part, p_part)


def solution(mesh):
    return jax.shard_map(
        on_device,
        mesh=mesh,
        in_specs=(
            P(None, ("wide", "narrow")),
            P(None, ("wide", "narrow")),
            P(("wide", "narrow")),
            P(None, ("wide", "narrow")),
            P(("wide", "narrow"), None),
            P(("wide", "narrow")),
        ),
        out_specs=P(None, ("wide", "narrow")),
        check_vma=False,
    )
```

time: 838 us -> 104 us (0.12)
  the two profiles are of different devices: /device:TPU:2 before, /device:TPU:4 now
where the time goes in v1:
time: 104 us
  Pallas kernels  92.7 us (89%)
  local copies, waits for them, and re-layouts  9.97 us (10%)
    pallas_call x1, Pallas kernels, tiles(): pl.pallas_call(tiles_kernel, out_shape=[jax.ShapeDtypeStruct((SLAB + 1, P...  39.4 us
    pallas_call x1, Pallas kernels, send_home(): pl.pallas_call(return_kernel, out_shape=jax.ShapeDtypeStruct((PORTS, BLK...  30.1 us
    pallas_call x1, Pallas kernels, fetch(): pl.pallas_call(fetch_kernel, out_shape=[jax.ShapeDtypeStruct((SLAB, ROWS,...  23.3 us
    unnamed x23, local copies, waits for them, and re-layouts  9.89 us

profile of v1, /device:TPU:4, one launch (start us, length us, event | category | flops | bytes accessed | tf_op | source)
XLA Modules:
  0.0 103.5 jit_solution(10744084655065973932)
XLA Ops:
  0.0 0.8 fusion
  0.8 0.1 reshape.8.pairs
  0.8 0.9 copy-done.4
  1.7 0.0 copy-start.5
  1.7 0.8 copy-done.5
  2.5 0.0 copy-start.6
  2.5 0.8 copy-done.6
  3.3 0.0 copy-start.9
  3.3 0.7 copy-done.9
  4.0 23.3 %shard_map.64 = (f32[32,24,256]{2,1,0:T(8,128)S(1)}, f32[64,24,256]{2,1,0:T(8,128)S(1)}, s32[40,32]{1,0:T(8,128)S(1)}, s32[40,32]{1,0:T(8,128)S(1)}, s32[8,128]{1,0:T(8,128)S(1)}) custom-call(f32[3,2048]{1,0:T(4,128)S(1)} %copy-done.5, f32[3,2048]{1,0:T(4,128)S(1)} %copy-done.6, f32[1,2048]{1,0:T(1,128)S(1)} %bitcast.1, f32[16,2048]{1,0:T(8,128)S(1)} %copy-done.4, ...), custom_call_target="tpu_custom_call" | custom-call | tf_op jit(solution)/shard_map/pallas_call | solution.py:176
  27.2 0.0 copy-start
  27.2 1.2 %copy-done = f32[64,24,256]{2,1,0:T(8,128)} copy-done((f32[64,24,256]{2,1,0:T(8,128)}, f32[64,24,256]{2,1,0:T(8,128)S(1)}, u32[]{:S(2)}) %copy-start) | copy-done | bytes 1572888
  28.4 0.0 copy-start.2
  28.4 0.9 copy-done.2
  29.3 0.0 copy-start.7
  29.3 0.6 copy-done.7
  29.9 0.0 copy-start.8
  29.9 0.6 copy-done.8
  30.5 0.6 copy-done.10
  31.1 39.4 %shard_map.65 = (f32[33,16,256]{2,1,0:T(8,128)}, f32[65,16,256]{2,1,0:T(8,128)}) custom-call(s32[8,128]{1,0:T(8,128)} %copy-done.10, s32[40,32]{1,0:T(8,128)} %copy-done.7, s32[40,32]{1,0:T(8,128)} %copy-done.8, f32[32,24,256]{2,1,0:T(8,128)} %copy-done.2, f32[64,24,256]{2,1,0:T(8,128)} %copy-done), custom_call_target="tpu_custom_call" | custom-call | tf_op jit(solution)/shard_map/pallas_call | solution.py:283
  70.4 1.2 %copy-done.1 = f32[65,16,256]{2,1,0:T(8,128)S(1)} copy-done((f32[65,16,256]{2,1,0:T(8,128)S(1)}, f32[65,16,256]{2,1,0:T(8,128)}, u32[]{:S(2)}) %copy-start.1) | copy-done | bytes 1064984
  71.7 1.0 %copy-done.3 = f32[33,16,256]{2,1,0:T(8,128)S(1)} copy-done((f32[33,16,256]{2,1,0:T(8,128)S(1)}, f32[33,16,256]{2,1,0:T(8,128)}, u32[]{:S(2)}) %copy-start.3) | copy-done | bytes 540696
  72.7 30.1 %shard_map.66 = f32[16,2048]{1,0:T(8,128)S(1)} custom-call(f32[33,16,256]{2,1,0:T(8,128)S(1)} %copy-done.3, f32[65,16,256]{2,1,0:T(8,128)S(1)} %copy-done.1), custom_call_target="tpu_custom_call" | custom-call | tf_op jit(solution)/shard_map/pallas_call | solution.py:360
  102.9 0.7 copy.8
  (4 shorter events, 0.0 us)
Async XLA Ops:
  0.8 0.9 copy-start.4
  1.7 0.8 copy-start.5
  2.5 0.8 copy-start.6
  3.3 0.7 copy-start.9
  27.2 1.2 %copy-start = (f32[64,24,256]{2,1,0:T(8,128)}, f32[64,24,256]{2,1,0:T(8,128)S(1)}, u32[]{:S(2)}) copy-start(f32[64,24,256]{2,1,0:T(8,128)S(1)} %get-tuple-element.16.par) | copy-start | bytes 4718596
  28.4 0.9 copy-start.2
  29.3 0.6 copy-start.7
  29.9 0.6 copy-start.8
  30.5 0.6 copy-start.10
  70.4 1.2 %copy-start.1 = (f32[65,16,256]{2,1,0:T(8,128)S(1)}, f32[65,16,256]{2,1,0:T(8,128)}, u32[]{:S(2)}) copy-start(f32[65,16,256]{2,1,0:T(8,128)} %get-tuple-element.18.p_part) | copy-start | bytes 3194884
  71.7 1.0 %copy-start.3 = (f32[33,16,256]{2,1,0:T(8,128)S(1)}, f32[33,16,256]{2,1,0:T(8,128)}, u32[]{:S(2)}) copy-start(f32[33,16,256]{2,1,0:T(8,128)} %get-tuple-element.17.s_part) | copy-start | bytes 1622020

commit v2 on v1

--- a/solution.py
+++ b/solution.py
@@ -18,7 +18,8 @@
 WINDOW = 2 * HOPS * BLK
 LIST = 40 * 32
 UNROLL = 8
-PARTS = 2
+PARTS = 4
+TILES_VMEM = 4 * 2**20
 f32 = jnp.float32
 bf16 = jnp.bfloat16
 MESH = pl.DeviceIdType.MESH
@@ -48,7 +49,7 @@
     )
 
 
-def list_pairs(rows, member, core, li_ref, lj_ref):
+def list_pairs(rows, member, core):
     lane = lax.broadcasted_iota(jnp.int32, (8, FIL), 1)
     row = lax.broadcasted_iota(jnp.int32, (8, FIL), 0)
     mine = (rows >= 0) & ((rows & 31) // BLK == member)
@@ -85,153 +86,195 @@
     used = flat < total
     li = jnp.where(diagonal, member * BLK + flat, jnp.where(used, out_i.astype(jnp.int32), SLAB))
     lj = jnp.where(diagonal, 2 * WINDOW + core * BLK + flat, jnp.where(used, out_j.astype(jnp.int32), WINDOW))
-    li_ref[...] = li
-    lj_ref[...] = lj
-    return total
+    return li, lj, total
+
+
+def directed(block):
+    cur = block[8:ROWS]
+    parts = jnp.concatenate([block[3 + comp : 4 + comp] * cur for comp in range(3)], axis=0)
+    head = parts.astype(bf16)
+    tail = (parts - head.astype(f32)).astype(bf16)
+    return jnp.concatenate([head, tail], axis=0)
+
+
+def columns(block, spread):
+    geometry = jnp.concatenate([block[0:3], block[6:7] * block[6:7]], axis=0)
+    head = geometry.astype(bf16).astype(f32)
+    rest = geometry - head
+    middle = rest.astype(bf16).astype(f32)
+    tail = rest - middle
+    terms = jnp.concatenate([head, middle, tail, jnp.zeros((4, FIL), f32)], axis=0)
+    return jnp.dot(terms.T.astype(bf16), spread, preferred_element_type=f32)
 
 
 def fetch_kernel(
-    pos, dirs, rad, cur, pairs, src, par, li_ref, lj_ref, n_ref,
-    own, lists, y_send, y_recv, l_send, l_recv, z_send, z_recv, c_send, c_recv, home_sem,
+    packed, pairs,
+    src, par, c_src, c_par, cols, table,
+    lists, y_send, y_recv, l_send, l_recv, z_send, z_recv, c_send, c_recv,
 ):
     wide, member, core, twin, ahead, behind = place()
     mates = [lax.rem(member + step, MEMBERS) for step in range(1, MEMBERS)]
     lists[...] = jnp.full((8, FIL), -1, jnp.int32)
     lists[pl.ds(member, 1)] = pairs[...]
+    for b in range(BLK):
+        block = packed[:, b * FIL : (b + 1) * FIL]
+        src[member * BLK + b] = block
+        par[core * BLK + b] = block
     greet([(wide, mate) for mate in mates] + [(ahead, member), (twin, member)])
-    for b in range(BLK):
-        cut = slice(b * FIL, (b + 1) * FIL)
-        own[b, 0:3] = pos[:, cut]
-        own[b, 3:6] = dirs[:, cut]
-        own[b, 6:7] = rad[:, cut]
-        own[b, 7:8] = rad[:, cut]
-        own[b, 8:ROWS] = cur[:, cut]
     half = BLK // PARTS
+    own = src.at[pl.ds(member * BLK, BLK)]
 
     def seat(hop, part):
         return pl.ds((2 * hop + core) * BLK + part * half, half)
 
-    sends = []
-    first = []
+    hops = [[]]
     for part in range(PARTS):
         copy = remote(
-            own.at[pl.ds(part * half, half)], par.at[seat(1, part)], z_send.at[0, part], z_recv.at[0, part], (behind, member)
+            src.at[pl.ds(member * BLK + part * half, half)], par.at[seat(1, part)],
+            z_send.at[0, part], z_recv.at[0, part], (behind, member),
         )
         copy.start()
-        first.append(copy)
-    hops = [first]
+        hops[0].append(copy)
     list_copies = []
     for step, mate in enumerate(mates):
-        copy = remote(
-            pairs, lists.at[pl.ds(member, 1)], l_send.at[step], l_recv.at[step], (wide, mate)
-        )
+        row = lists.at[pl.ds(member, 1)]
+        copy = remote(row, row, l_send.at[step], l_recv.at[step], (wide, mate))
         copy.start()
         list_copies.append(copy)
     unit_copies = []
     for step, mate in enumerate(mates):
-        copy = remote(own, src.at[pl.ds(member * BLK, BLK)], y_send.at[step], y_recv.at[step], (wide, mate))
+        copy = remote(own, own, y_send.at[step], y_recv.at[step], (wide, mate))
         copy.start()
         unit_copies.append(copy)
-    core_copies = []
+    core_copies = {}
     copy = remote(own, par.at[pl.ds(core * BLK, BLK)], c_send.at[0, 0], c_recv.at[0, 0], (twin, member))
     copy.start()
-    core_copies.append(copy)
-    home = [
-        pltpu.make_async_copy(own, src.at[pl.ds(member * BLK, BLK)], home_sem.at[0]),
-        pltpu.make_async_copy(own, par.at[pl.ds(core * BLK, BLK)], home_sem.at[1]),
-    ]
-    for copy in home:
-        copy.start()
-    for copy in list_copies:
-        copy.wait()
-    total = list_pairs(lists[...], member, core, li_ref, lj_ref)
-    n_ref[...] = jnp.broadcast_to(total, (8, 128))
-    for hop in range(1, HOPS):
+    core_copies[0, 0] = copy
+
+    term = lax.broadcasted_iota(jnp.int32, (16, 512), 0)
+    group = lax.broadcasted_iota(jnp.int32, (16, 512), 1) // 128
+    spread = jnp.where((term < 12) & (lax.rem(term, 4) == group), 1.0, 0.0).astype(bf16)
+
+    def ready_sources(first):
+        @pl.loop(0, BLK // 4)
+        def _(quad):
+            for b in range(4):
+                i = first + 4 * quad + b
+                block = src[i]
+                c_src[i] = directed(block)
+                wide_columns = columns(block, spread)
+                for q in range(4):
+                    cols[i, q] = wide_columns[:, q * 128 : (q + 1) * 128]
+
+    def ready_partners(first, count_of):
+        @pl.loop(0, count_of // 2)
+        def _(duo):
+            for b in range(2):
+                j = first + 2 * duo + b
+                c_par[j] = directed(par[j])
+
+    def pass_on(hop):
         later = []
         for part in range(PARTS):
             hops[hop - 1][part].wait_recv()
             if hop < HOPS - 1:
                 copy = remote(
-                    par.at[seat(hop, part)], par.at[seat(hop + 1, part)], z_send.at[hop, part], z_recv.at[hop, part], (behind, member)
+                    par.at[seat(hop, part)], par.at[seat(hop + 1, part)],
+                    z_send.at[hop, part], z_recv.at[hop, part], (behind, member),
                 )
                 copy.start()
                 later.append(copy)
             copy = remote(
-                par.at[seat(hop, part)], par.at[seat(hop, part)], c_send.at[hop, part], c_recv.at[hop, part], (twin, member)
+                par.at[seat(hop, part)], par.at[seat(hop, part)],
+                c_send.at[hop, part], c_recv.at[hop, part], (twin, member),
             )
             copy.start()
-            core_copies.append(copy)
+            core_copies[hop, part] = copy
         hops.append(later)
-    for group in hops:
-        for copy in group:
+
+    def from_core(hop):
+        for part in range(PARTS if hop else 1):
+            core_copies[hop, part].wait_recv()
+
+    def mate_of(step):
+        return lax.rem(member + MEMBERS - 1 - step, MEMBERS)
+
+    ready_sources(member * BLK)
+    for copy in list_copies:
+        copy.wait()
+    li, lj, total = list_pairs(lists[...], member, core)
+    table[0:40] = li
+    table[40:80] = lj
+    table[80:88] = jnp.broadcast_to(total, (8, 32))
+    pass_on(1)
+    for step in (0, 2):
+        unit_copies[step].wait_recv()
+        ready_sources(mate_of(step) * BLK)
+    pass_on(2)
+    unit_copies[1].wait_recv()
+    ready_sources(mate_of(1) * BLK)
+    from_core(0)
+    ready_partners(0, 2 * BLK)
+    from_core(1)
+    ready_partners(2 * BLK, 2 * BLK)
+    pass_on(3)
+    from_core(2)
+    ready_partners(4 * BLK, 2 * BLK)
+    ready_partners((6 + core) * BLK, BLK)
+    from_core(3)
+    ready_partners((7 - core) * BLK, BLK)
+    for group_of in hops:
+        for copy in group_of:
             copy.wait_send()
-    for copy in unit_copies + core_copies + home:
-        copy.wait()
-
-
-def fetch(pos, dirs, rad, cur, pairs):
+    for copy in unit_copies + list(core_copies.values()):
+        copy.wait_send()
+
+
+def fetch(packed, pairs):
     vm = pl.BlockSpec(memory_space=pltpu.VMEM)
-    hbm = pl.BlockSpec(memory_space=pl.ANY)
     dma = pltpu.SemaphoreType.DMA
     return pl.pallas_call(
         fetch_kernel,
         out_shape=[
             jax.ShapeDtypeStruct((SLAB, ROWS, FIL), f32),
             jax.ShapeDtypeStruct((WINDOW, ROWS, FIL), f32),
-            jax.ShapeDtypeStruct((40, 32), jnp.int32),
-            jax.ShapeDtypeStruct((40, 32), jnp.int32),
-            jax.ShapeDtypeStruct((8, 128), jnp.int32),
+            jax.ShapeDtypeStruct((SLAB, 6 * PORTS, FIL), bf16),
+            jax.ShapeDtypeStruct((WINDOW, 6 * PORTS, FIL), bf16),
+            jax.ShapeDtypeStruct((SLAB, 4, FIL, 128), f32),
+            jax.ShapeDtypeStruct((88, 32), jnp.int32),
         ],
-        in_specs=[vm] * 5,
-        out_specs=[hbm, hbm, vm, vm, vm],
+        in_specs=[vm] * 2,
+        out_specs=[vm] * 6,
         scratch_shapes=[
-            pltpu.VMEM((BLK, ROWS, FIL), f32),
             pltpu.VMEM((8, FIL), jnp.int32),
             dma((3,)), dma((3,)), dma((3,)), dma((3,)),
             dma((3, PARTS)), dma((3, PARTS)),
             dma((HOPS, PARTS)), dma((HOPS, PARTS)),
-            dma((2,)),
         ],
         compiler_params=pltpu.CompilerParams(
-            collective_id=0, has_side_effects=True, vmem_limit_bytes=32 * 2**20
+            collective_id=0, has_side_effects=True, vmem_limit_bytes=8 * 2**20
         ),
-    )(pos, dirs, rad, cur, pairs)
-
-
-def directed(block):
-    cur = block[8:ROWS]
-    parts = jnp.concatenate([block[3 + comp : 4 + comp] * cur for comp in range(3)], axis=0)
-    head = parts.astype(bf16)
-    tail = (parts - head.astype(f32)).astype(bf16)
-    return jnp.concatenate([head, tail], axis=0)
-
-
-def tiles_kernel(n_ref, li_ref, lj_ref, src, par, s_out, p_out, c_src, c_par, cols, even, odd):
-    n = n_ref[0, 0]
-
-    @pl.loop(0, SLAB)
+    )(packed, pairs)
+
+
+def tiles_kernel(table, src, par, c_src, c_par, cols, s_out, p_out, even, odd, turns, sem):
+    load = pltpu.make_async_copy(table, turns, sem)
+    load.start()
+
+    @pl.loop(0, SLAB + 1)
     def _(i):
-        block = src[i]
-        c_src[i] = directed(block)
         s_out[i] = jnp.zeros((PORTS, FIL), f32)
-        turned = block[0:8].T
-        for place_of, row in enumerate((0, 1, 2, 6)):
-            column = turned[:, row : row + 1]
-            if row == 6:
-                column = column * column
-            cols[i, place_of] = jnp.broadcast_to(column, (FIL, 128))
-
-    @pl.loop(0, WINDOW)
+
+    @pl.loop(0, WINDOW + 1)
     def _(j):
-        c_par[j] = directed(par[j])
         p_out[j] = jnp.zeros((PORTS, FIL), f32)
 
-    s_out[SLAB] = jnp.zeros((PORTS, FIL), f32)
-    p_out[WINDOW] = jnp.zeros((PORTS, FIL), f32)
+    load.wait()
+    n = turns[80, 0]
 
     def pair(k):
         row, col = k // 32, k & 31
-        i, j = li_ref[row, col], lj_ref[row, col]
+        i, j = turns[row, col], turns[40 + row, col]
         return i, jnp.minimum(i, SLAB - 1), jnp.minimum(j, WINDOW), j & (WINDOW - 1)
 
     def chunks(k, buf):
@@ -277,8 +320,7 @@
             step(k + q + 1, later, k + q, now)
 
 
-def tiles(n, li, lj, src, par):
-    sm = pl.BlockSpec(memory_space=pltpu.SMEM)
+def tiles(table, src, par, c_src, c_par, cols):
     vm = pl.BlockSpec(memory_space=pltpu.VMEM)
     return pl.pallas_call(
         tiles_kernel,
@@ -286,17 +328,16 @@
             jax.ShapeDtypeStruct((SLAB + 1, PORTS, FIL), f32),
             jax.ShapeDtypeStruct((WINDOW + 1, PORTS, FIL), f32),
         ],
-        in_specs=[sm, sm, sm, vm, vm],
-        out_specs=[vm, vm],
+        in_specs=[vm] * 6,
+        out_specs=[vm] * 2,
         scratch_shapes=[
-            pltpu.VMEM((SLAB, 6 * PORTS, FIL), bf16),
-            pltpu.VMEM((WINDOW, 6 * PORTS, FIL), bf16),
-            pltpu.VMEM((SLAB, 4, FIL, 128), f32),
             pltpu.VMEM((FIL, FIL), bf16),
             pltpu.VMEM((FIL, FIL), bf16),
+            pltpu.SMEM((88, 32), jnp.int32),
+            pltpu.SemaphoreType.DMA,
         ],
-        compiler_params=pltpu.CompilerParams(vmem_limit_bytes=56 * 2**20),
-    )(n, li, lj, src, par)
+        compiler_params=pltpu.CompilerParams(vmem_limit_bytes=TILES_VMEM),
+    )(table, src, par, c_src, c_par, cols)
 
 
 def return_kernel(
@@ -372,16 +413,19 @@
             dma((HOPS, PARTS)), dma((HOPS, PARTS)),
         ],
         compiler_params=pltpu.CompilerParams(
-            collective_id=1, has_side_effects=True, vmem_limit_bytes=32 * 2**20
+            collective_id=1, has_side_effects=True, vmem_limit_bytes=8 * 2**20
         ),
     )(s_part, p_part)
 
 
 def on_device(positions, directions, radius, currents, pair_target, pair_count):
+    rad = radius.reshape(1, BLK * FIL)
+    packed = jnp.concatenate([positions, directions, rad, rad, currents], axis=0)
     slots = jnp.arange(MAXP, dtype=jnp.int32)
     pairs = jnp.where(slots[None, :] < pair_count[:, None], pair_target, -1).reshape(1, BLK * MAXP)
-    src, par, li, lj, n = fetch(positions, directions, radius.reshape(1, BLK * FIL), currents, pairs)
-    s_part, p_part = tiles(n, li, lj, src, par)
+    fetched = fetch(packed, pairs)
+    src, par, c_src, c_par, cols, table = fetched
+    s_part, p_part = tiles(table, src, par, c_src, c_par, cols)
     return send_home(s_part, p_part)
 
 

time: 104 us -> 84.4 us (0.81)
  the two profiles are of different devices: /device:TPU:4 before, /device:TPU:7 now
where the time goes in v2:
time: 84.4 us; the launch traced here: 84.1 us
  Pallas kernels  80.9 us (96%)
  local copies, waits for them, and re-layouts  2.48 us (3%)
    pallas_call x1, Pallas kernels, send_home(): pl.pallas_call(return_kernel, out_shape=jax.ShapeDtypeStruct((PORTS, BLK...  34.7 us
    pallas_call x1, Pallas kernels, fetch(): pl.pallas_call(fetch_kernel, out_shape=[jax.ShapeDtypeStruct((SLAB, ROWS,...  26.3 us
    pallas_call x1, Pallas kernels, tiles(): pl.pallas_call(tiles_kernel, out_shape=[jax.ShapeDtypeStruct((SLAB + 1, P...  19.9 us
    concatenate x1, local copies, waits for them, and re-layouts, on_device(): jnp.concatenate([positions, directions, rad, rad, currents], axis=0)  1.74 us

profile of v2, /device:TPU:7, one launch (start us, length us, event | category | flops | bytes accessed | tf_op | source)
XLA Modules:
  0.0 84.1 jit_solution(17511962343338385053)
XLA Ops:
  0.0 0.8 fusion
  0.8 0.1 reshape.8.pairs
  0.8 1.7 %concatenate.3.packed = f32[24,2048]{1,0:T(8,128)S(1)} concatenate(f32[3,2048]{1,0:T(4,128)} %param.6, f32[3,2048]{1,0:T(4,128)} %param.7, f32[1,2048]{1,0:T(1,128)} %bitcast.1, f32[1,2048]{1,0:T(1,128)} %bitcast.2, f32[16,2048]{1,0:T(8,128)} %param.9), dimensions={0} | concatenate | bytes 393216 | tf_op jit(solution)/shard_map/concatenate | solution.py:423
  2.6 26.3 %shard_map.64 = (f32[32,24,256]{2,1,0:T(8,128)S(1)}, f32[64,24,256]{2,1,0:T(8,128)S(1)}, bf16[32,96,256]{2,1,0:T(8,128)(2,1)S(1)}, bf16[64,96,256]{2,1,0:T(8,128...) custom-call(f32[24,2048]{1,0:T(8,128)S(1)} %concatenate.3.packed, s32[1,256]{1,0:T(1,128)S(1)} %reshape.8.pairs), custom_call_target="tpu_custom_call" | custom-call | tf_op jit(solution)/shard_map/pallas_call | solution.py:236
  28.9 19.9 %shard_map.65 = (f32[33,16,256]{2,1,0:T(8,128)S(1)}, f32[65,16,256]{2,1,0:T(8,128)S(1)}) custom-call(s32[88,32]{1,0:T(8,128)S(1)} %get-tuple-element.13.table, f32[32,24,256]{2,1,0:T(8,128)S(1)} %get-tuple-element.14.src, f32[64,24,256]{2,1,0:T(8,128)S(1)} %get-tuple-element.15.par, bf16[32,96,256]{2,1,0:T(8,128)(2,1)S(1)} %get-tuple-element.16.c_src, ...), custom_call_target="tpu_custom_call" | custom-call | tf_op jit(solution)/shard_map/pallas_call | solution.py:325
  48.8 34.7 %shard_map.66 = f32[16,2048]{1,0:T(8,128)S(1)} custom-call(f32[33,16,256]{2,1,0:T(8,128)S(1)} %get-tuple-element.19.s_part, f32[65,16,256]{2,1,0:T(8,128)S(1)} %get-tuple-element.20.p_part), custom_call_target="tpu_custom_call" | custom-call | tf_op jit(solution)/shard_map/pallas_call | solution.py:401
  83.5 0.7 copy.8

commit v3 on v2

v3 whole, which is shorter than its diff:
```python
import functools

import jax
import jax.numpy as jnp
from jax import lax
from jax.experimental import pallas as pl
from jax.experimental.pallas import tpu as pltpu
from jax.sharding import PartitionSpec as P

FIL = 256
PORTS = 16
BLK = 8
MAXP = 32
SLAB = 32
MEMBERS = 4
HOPS = 4
ROWS = 24
WINDOW = 2 * HOPS * BLK
ALL = SLAB + WINDOW
LIST = 40
UNROLL = 8
PARTS = 4
TILES_VMEM = 4 * 2**20
f32 = jnp.float32
bf16 = jnp.bfloat16
MESH = pl.DeviceIdType.MESH


def place():
    wide = lax.axis_index("wide")
    member = lax.axis_index("narrow")
    count = lax.axis_size("wide")
    core = lax.rem(wide, 2)
    twin = wide + 1 - 2 * core
    ahead = lax.rem(wide + 2, count)
    behind = lax.rem(wide + count - 2, count)
    return wide, member, core, twin, ahead, behind


def greet(devices):
    barrier = pltpu.get_barrier_semaphore()
    for device in devices:
        pl.semaphore_signal(barrier, inc=1, device_id=device, device_id_type=MESH)
    pl.semaphore_wait(barrier, len(devices))


def remote(src, dst, send, recv, device):
    return pltpu.make_async_remote_copy(
        src_ref=src, dst_ref=dst, send_sem=send, recv_sem=recv, device_id=device, device_id_type=MESH
    )


def list_pairs(rows, member, core):
    lane = lax.broadcasted_iota(jnp.int32, (8, FIL), 1)
    row = lax.broadcasted_iota(jnp.int32, (8, FIL), 0)
    which = lax.broadcasted_iota(jnp.int32, (8, 1), 0)
    home = which < MEMBERS
    upper = (
        lax.broadcasted_iota(jnp.int32, (FIL, FIL), 0) <= lax.broadcasted_iota(jnp.int32, (FIL, FIL), 1)
    ).astype(bf16)

    def by_row(chosen):
        return jnp.sum(chosen.astype(jnp.int32), axis=1, keepdims=True)

    def by_slab(chosen):
        counts = by_row(chosen)
        own = jnp.sum(jnp.where(home, counts, 0), axis=0, keepdims=True)
        twin = jnp.sum(jnp.where(home, 0, counts), axis=0, keepdims=True)
        return own, twin

    def rank(chosen, apart):
        inclusive = jnp.dot(chosen.astype(f32).astype(bf16), upper, preferred_element_type=f32)
        counts = by_row(chosen)
        base = jnp.zeros((8, 1), jnp.int32)
        for m in range(7):
            later = which > m
            if apart:
                later = later & (home == (m < MEMBERS))
            base = base + jnp.where(later, counts[m : m + 1], 0)
        return base + inclusive.astype(jnp.int32) - 1

    valid = rows >= 0
    offset = rows // SLAB
    quarter = (rows & (SLAB - 1)) // BLK
    source = (row & (MEMBERS - 1)) * BLK + lane // MAXP
    free = valid & (offset == 0)
    fixed = valid & (offset > 0)
    shares = [by_slab(fixed & (quarter == q)) for q in range(MEMBERS)]
    free_total = by_slab(free)
    begin, width = [], []
    for slab in range(2):
        known = [share[slab] for share in shares]
        level = (known[0] + known[1] + known[2] + known[3] + free_total[slab] + MEMBERS - 1) // MEMBERS
        room = [jnp.maximum(level - share, 0) for share in known]
        first = jnp.zeros((1, 1), jnp.int32)
        span = jnp.zeros((1, 1), jnp.int32)
        for q in range(MEMBERS):
            first = first + jnp.where(member > q, room[q], 0)
            span = span + jnp.where(member == q, room[q], 0)
        begin.append(first)
        width.append(span)
    begins = jnp.where(home, begin[0], begin[1])
    ends = begins + jnp.where(home, width[0], width[1])
    free_rank = rank(free, True)
    dealt = (fixed & (quarter == member)) | (free & (free_rank >= begins) & (free_rank < ends))
    loads = by_slab(dealt)
    movable = dealt & (quarter == member) & (source // BLK == member)
    movable_rank = rank(movable, True)
    give = jnp.maximum(loads[0] - loads[1], 0) // 2
    take = jnp.maximum(loads[1] - loads[0], 0) // 2
    crosses = movable & (movable_rank < jnp.where(home, give, take))
    mine = (dealt & home & ~crosses) | (crosses & ~home)
    spot = rank(mine, False)
    total = jnp.sum(by_row(mine), axis=0, keepdims=True)
    there = jnp.where(home, core, 1 - core)
    in_window = SLAB + (there + offset) * BLK + (rows & (BLK - 1))
    partner = jnp.where(home & (offset == 0), rows & (SLAB - 1), in_window)
    source = jnp.where(home, source, SLAB + there * BLK + (source & (BLK - 1)))
    high = jnp.where(mine, spot // 32, -1)
    low = jnp.where(mine, spot & 31, -1)
    out_i = jnp.zeros((LIST, 32), f32)
    out_j = jnp.zeros((LIST, 32), f32)
    spots_high = lax.broadcasted_iota(jnp.int32, (LIST, FIL), 0)
    spots_low = lax.broadcasted_iota(jnp.int32, (32, FIL), 0)
    contract = (((1,), (1,)), ((), ()))
    for m in range(8):
        pick_high = spots_high == high[m : m + 1]
        pick_low = (spots_low == low[m : m + 1]).astype(f32).astype(bf16)
        put_i = jnp.where(pick_high, source[m : m + 1].astype(f32), 0.0).astype(bf16)
        put_j = jnp.where(pick_high, partner[m : m + 1].astype(f32), 0.0).astype(bf16)
        out_i = out_i + lax.dot_general(put_i, pick_low, contract, preferred_element_type=f32)
        out_j = out_j + lax.dot_general(put_j, pick_low, contract, preferred_element_type=f32)
    flat = 32 * lax.broadcasted_iota(jnp.int32, (LIST, 32), 0) + lax.broadcasted_iota(jnp.int32, (LIST, 32), 1)
    used = flat < total
    li = jnp.where(used, out_i.astype(jnp.int32), ALL)
    lj = jnp.where(used, out_j.astype(jnp.int32), ALL)
    return li, lj, total


def directed(block):
    cur = block[8:ROWS]
    parts = jnp.concatenate([block[3 + comp : 4 + comp] * cur for comp in range(3)], axis=0)
    head = parts.astype(bf16)
    tail = (parts - head.astype(f32)).astype(bf16)
    return jnp.concatenate([head, tail], axis=0)


def columns(block, spread):
    geometry = jnp.concatenate([block[0:3], block[6:7] * block[6:7]], axis=0)
    head = geometry.astype(bf16).astype(f32)
    rest = geometry - head
    middle = rest.astype(bf16).astype(f32)
    tail = rest - middle
    terms = jnp.concatenate([head, middle, tail, jnp.zeros((4, FIL), f32)], axis=0)
    return jnp.dot(terms.T.astype(bf16), spread, preferred_element_type=f32)


def tile_pieces(cols, i, geometry, buf):
    radius = geometry[6:7] * geometry[6:7]

    def piece(h, r):
        cut = slice(h * 128, h * 128 + 128)
        xb, yb, zb = [jnp.broadcast_to(geometry[q : q + 1, cut], (16, 128)) for q in range(3)]
        rb = jnp.broadcast_to(radius[:, cut], (16, 128))
        xa, ya, za, ra = [cols[i, q, r : r + 16, :] for q in range(4)]
        dx, dy, dz = xa - xb, ya - yb, za - zb
        gap = (ra + rb) + dx * dx + dy * dy + dz * dz
        buf[r : r + 16, cut] = lax.rsqrt(gap).astype(bf16)

    return [functools.partial(piece, h, r) for h in range(2) for r in range(0, FIL, 16)]


def fold(product, dirs):
    both = product[0 : 3 * PORTS] + product[3 * PORTS : 6 * PORTS]
    return (
        both[0:PORTS] * dirs[0:1] + both[PORTS : 2 * PORTS] * dirs[1:2]
    ) + both[2 * PORTS : 3 * PORTS] * dirs[2:3]


def fetch_kernel(
    packed, pairs,
    blocks, terms, cols, acc, table,
    lists, tile, t_send, t_recv, y_send, y_recv, l_send, l_recv, z_send, z_recv, c_send, c_recv,
):
    wide, member, core, twin, ahead, behind = place()
    mates = [lax.rem(member + step, MEMBERS) for step in range(1, MEMBERS)]
    lists[...] = jnp.full((8, FIL), -1, jnp.int32)
    lists[pl.ds(member, 1)] = pairs[...]
    for b in range(BLK):
        block = packed[:, b * FIL : (b + 1) * FIL]
        blocks[member * BLK + b] = block
        blocks[SLAB + core * BLK + b] = block
    greet([(wide, mate) for mate in mates] + [(ahead, member), (twin, member)])
    half = BLK // PARTS
    own = blocks.at[pl.ds(member * BLK, BLK)]

    def seat(hop, part):
        return pl.ds(SLAB + (2 * hop + core) * BLK + part * half, half)

    hops = [[]]
    for part in range(PARTS):
        copy = remote(
            blocks.at[pl.ds(member * BLK + part * half, half)], blocks.at[seat(1, part)],
            z_send.at[0, part], z_recv.at[0, part], (behind, member),
        )
        copy.start()
        hops[0].append(copy)
    list_copies = []
    for step, mate in enumerate(mates):
        row = lists.at[pl.ds(member, 1)]
        copy = remote(row, row, l_send.at[step], l_recv.at[step], (wide, mate))
        copy.start()
        list_copies.append(copy)
    unit_copies = []
    for step, mate in enumerate(mates):
        copy = remote(own, own, y_send.at[step], y_recv.at[step], (wide, mate))
        copy.start()
        unit_copies.append(copy)
    core_copies = {}
    copy = remote(own, blocks.at[pl.ds(SLAB + core * BLK, BLK)], c_send.at[0, 0], c_recv.at[0, 0], (twin, member))
    copy.start()
    core_copies[0, 0] = copy

    term = lax.broadcasted_iota(jnp.int32, (16, 512), 0)
    group = lax.broadcasted_iota(jnp.int32, (16, 512), 1) // 128
    spread = jnp.where((term < 12) & (lax.rem(term, 4) == group), 1.0, 0.0).astype(bf16)

    def ready_sources(first, held):
        @pl.loop(0, BLK // 4)
        def _(quad):
            for b in range(4):
                i = first + 4 * quad + b
                block = blocks[i]
                terms[i] = directed(block)
                wide_columns = columns(block, spread)
                for q in range(4):
                    cols[held + 4 * quad + b, q] = wide_columns[:, q * 128 : (q + 1) * 128]

    def ready_partners(first, count_of):
        @pl.loop(0, count_of // 2)
        def _(duo):
            for b in range(2):
                j = SLAB + first + 2 * duo + b
                terms[j] = directed(blocks[j])

    def pass_on(hop):
        later = []
        for part in range(PARTS):
            hops[hop - 1][part].wait_recv()
            if hop < HOPS - 1:
                copy = remote(
                    blocks.at[seat(hop, part)], blocks.at[seat(hop + 1, part)],
                    z_send.at[hop, part], z_recv.at[hop, part], (behind, member),
                )
                copy.start()
                later.append(copy)
            copy = remote(
                blocks.at[seat(hop, part)], blocks.at[seat(hop, part)],
                c_send.at[hop, part], c_recv.at[hop, part], (twin, member),
            )
            copy.start()
            core_copies[hop, part] = copy
        hops.append(later)

    def from_core(hop):
        for part in range(PARTS if hop else 1):
            core_copies[hop, part].wait_recv()

    def mate_of(step):
        return lax.rem(member + MEMBERS - 1 - step, MEMBERS)

    @pl.loop(0, ALL + 1)
    def _(i):
        acc[i] = jnp.zeros((PORTS, FIL), f32)

    ready_sources(member * BLK, member * BLK)
    for copy in list_copies:
        copy.wait()
    twin_lists = remote(
        lists.at[pl.ds(0, MEMBERS)], lists.at[pl.ds(MEMBERS, MEMBERS)], t_send, t_recv, (twin, member)
    )
    twin_lists.start()
    pass_on(1)
    twin_lists.wait()
    li, lj, total = list_pairs(lists[...], member, core)
    table[0:LIST] = li
    table[LIST : 2 * LIST] = lj
    table[2 * LIST : 2 * LIST + 8] = jnp.broadcast_to(total, (8, 32))
    for step in (0, 2):
        unit_copies[step].wait_recv()
        ready_sources(mate_of(step) * BLK, mate_of(step) * BLK)
    pass_on(2)
    unit_copies[1].wait_recv()
    ready_sources(mate_of(1) * BLK, mate_of(1) * BLK)

    @pl.loop(0, BLK)
    def _(b):
        i = member * BLK + b
        for piece in tile_pieces(cols, i, blocks[i, 0:8, :], tile):
            piece()
        product = lax.dot_general(terms[i], tile[...], (((1,), (1,)), ((), ())), preferred_element_type=f32)
        acc[i] = fold(product, blocks[i, 3:6, :])

    from_core(0)
    ready_sources(SLAB + (1 - core) * BLK, SLAB)
    ready_partners(core * BLK, BLK)
    from_core(1)
    ready_partners(2 * BLK, 2 * BLK)
    pass_on(3)
    from_core(2)
    ready_partners(4 * BLK, 2 * BLK)
    ready_partners((6 + core) * BLK, BLK)
    from_core(3)
    ready_partners((7 - core) * BLK, BLK)
    for group_of in hops:
        for copy in group_of:
            copy.wait_send()
    for copy in unit_copies + list(core_copies.values()):
        copy.wait_send()


def fetch(packed, pairs):
    vm = pl.BlockSpec(memory_space=pltpu.VMEM)
    dma = pltpu.SemaphoreType.DMA
    return pl.pallas_call(
        fetch_kernel,
        out_shape=[
            jax.ShapeDtypeStruct((ALL, ROWS, FIL), f32),
            jax.ShapeDtypeStruct((ALL, 6 * PORTS, FIL), bf16),
            jax.ShapeDtypeStruct((SLAB + BLK, 4, FIL, 128), f32),
            jax.ShapeDtypeStruct((ALL + 1, PORTS, FIL), f32),
            jax.ShapeDtypeStruct((88, 32), jnp.int32),
        ],
        in_specs=[vm] * 2,
        out_specs=[vm] * 5,
        scratch_shapes=[
            pltpu.VMEM((8, FIL), jnp.int32),
            pltpu.VMEM((FIL, FIL), bf16),
            dma, dma,
            dma((3,)), dma((3,)), dma((3,)), dma((3,)),
            dma((3, PARTS)), dma((3, PARTS)),
            dma((HOPS, PARTS)), dma((HOPS, PARTS)),
        ],
        compiler_params=pltpu.CompilerParams(
            collective_id=0, has_side_effects=True, vmem_limit_bytes=8 * 2**20
        ),
    )(packed, pairs)


def tiles_kernel(table, blocks, terms, cols, start, acc, even, odd, turns, sem):
    load = pltpu.make_async_copy(table, turns, sem)
    load.start()
    load.wait()
    n = turns[2 * LIST, 0]

    def pair(k):
        row, col = k // 32, k & 31
        return turns[row, col], turns[LIST + row, col]

    def chunks(k, buf):
        i, j = pair(k)
        held = jnp.where(i < SLAB, i, SLAB + (i & (BLK - 1)))
        return tile_pieces(cols, held, blocks[jnp.minimum(j, ALL - 1), 0:8, :], buf)

    def step(k_next, buf_next, k, buf):
        work = chunks(k_next, buf_next)
        i_put, j_put = pair(k)
        i, j = jnp.minimum(i_put, ALL - 1), jnp.minimum(j_put, ALL - 1)
        behind = lax.dot_general(terms[i], buf[...], (((1,), (0,)), ((), ())), preferred_element_type=f32)
        for piece in work[:16]:
            piece()
        acc[j_put] += fold(behind, blocks[j, 3:6, :])
        ahead = lax.dot_general(terms[j], buf[...], (((1,), (1,)), ((), ())), preferred_element_type=f32)
        for piece in work[16:]:
            piece()
        acc[i_put] += fold(ahead, blocks[i, 3:6, :])

    for piece in chunks(0, even):
        piece()

    @pl.loop(0, (n + UNROLL - 1) // UNROLL)
    def _(turn):
        k = UNROLL * turn
        for q in range(UNROLL):
            now, later = (even, odd) if q % 2 == 0 else (odd, even)
            step(k + q + 1, later, k + q, now)


def tiles(table, blocks, terms, cols, acc):
    vm = pl.BlockSpec(memory_space=pltpu.VMEM)
    return pl.pallas_call(
        tiles_kernel,
        out_shape=jax.ShapeDtypeStruct((ALL + 1, PORTS, FIL), f32),
        in_specs=[vm] * 5,
        out_specs=vm,
        scratch_shapes=[
            pltpu.VMEM((FIL, FIL), bf16),
            pltpu.VMEM((FIL, FIL), bf16),
            pltpu.SMEM((88, 32), jnp.int32),
            pltpu.SemaphoreType.DMA,
        ],
        input_output_aliases={4: 0},
        compiler_params=pltpu.CompilerParams(vmem_limit_bytes=TILES_VMEM),
    )(table, blocks, terms, cols, acc)


def return_kernel(
    acc, out, x_buf, y_buf, z_buf, z_out, y_send, y_recv, z_send, z_recv, c_send, c_recv
):
    wide, member, core, twin, ahead, behind = place()
    mates = [lax.rem(member + step, MEMBERS) for step in range(1, MEMBERS)]
    greet([(wide, mate) for mate in mates] + [(behind, member), (twin, member)])
    half = BLK // PARTS
    core_copies = {}
    for hop in range(HOPS - 1, -1, -1):
        for part in range(PARTS):
            copy = remote(
                acc.at[pl.ds(SLAB + (2 * hop + 1 - core) * BLK + part * half, half)],
                x_buf.at[hop, pl.ds(part * half, half)],
                c_send.at[hop, part], c_recv.at[hop, part], (twin, member),
            )
            copy.start()
            core_copies[hop, part] = copy
    unit_copies = []
    for step, mate in enumerate(mates):
        copy = remote(
            acc.at[pl.ds(mate * BLK, BLK)], y_buf.at[step], y_send.at[step], y_recv.at[step], (wide, mate)
        )
        copy.start()
        unit_copies.append(copy)
    hops = {}
    for hop in range(HOPS - 1, -1, -1):
        for part in range(PARTS):
            cut = pl.ds(part * half, half)
            core_copies[hop, part].wait_recv()
            value = x_buf[hop, cut] + acc[pl.ds(SLAB + (2 * hop + core) * BLK + part * half, half)]
            if hop < HOPS - 1:
                hops[hop + 1, part].wait_recv()
                value = value + z_buf[hop, cut]
            if hop > 0:
                z_out[hop - 1, cut] = value
                copy = remote(
                    z_out.at[hop - 1, cut], z_buf.at[hop - 1, cut],
                    z_send.at[hop - 1, part], z_recv.at[hop - 1, part], (ahead, member),
                )
                copy.start()
                hops[hop, part] = copy
            else:
                if part == 0:
                    for copy in unit_copies:
                        copy.wait_recv()
                value = value + acc[pl.ds(member * BLK + part * half, half)]
                for step in range(MEMBERS - 1):
                    value = value + y_buf[step, cut]
                for b in range(half):
                    at = (part * half + b) * FIL
                    out[:, at : at + FIL] = value[b]
    for copy in list(core_copies.values()) + unit_copies + list(hops.values()):
        copy.wait_send()


def send_home(acc):
    vm = pl.BlockSpec(memory_space=pltpu.VMEM)
    dma = pltpu.SemaphoreType.DMA
    return pl.pallas_call(
        return_kernel,
        out_shape=jax.ShapeDtypeStruct((PORTS, BLK * FIL), f32),
        in_specs=[vm],
        out_specs=vm,
        scratch_shapes=[
            pltpu.VMEM((HOPS, BLK, PORTS, FIL), f32),
            pltpu.VMEM((MEMBERS - 1, BLK, PORTS, FIL), f32),
            pltpu.VMEM((HOPS - 1, BLK, PORTS, FIL), f32),
            pltpu.VMEM((HOPS - 1, BLK, PORTS, FIL), f32),
            dma((3,)), dma((3,)),
            dma((HOPS - 1, PARTS)), dma((HOPS - 1, PARTS)),
            dma((HOPS, PARTS)), dma((HOPS, PARTS)),
        ],
        compiler_params=pltpu.CompilerParams(
            collective_id=1, has_side_effects=True, vmem_limit_bytes=8 * 2**20
        ),
    )(acc)


def on_device(positions, directions, radius, currents, pair_target, pair_count):
    rad = radius.reshape(1, BLK * FIL)
    packed = jnp.concatenate([positions, directions, rad, rad, currents], axis=0)
    slots = jnp.arange(MAXP, dtype=jnp.int32)
    pairs = jnp.where(slots[None, :] < pair_count[:, None], pair_target, -1).reshape(1, BLK * MAXP)
    blocks, terms, cols, acc, table = fetch(packed, pairs)
    return send_home(tiles(table, blocks, terms, cols, acc))


def solution(mesh):
    return jax.shard_map(
        on_device,
        mesh=mesh,
        in_specs=(
            P(None, ("wide", "narrow")),
            P(None, ("wide", "narrow")),
            P(("wide", "narrow")),
            P(None, ("wide", "narrow")),
            P(("wide", "narrow"), None),
            P(("wide", "narrow")),
        ),
        out_specs=P(None, ("wide", "narrow")),
        check_vma=False,
    )
```

time: 84.4 us -> 77.8 us (0.922)
  the two profiles are of different devices: /device:TPU:7 before, /device:TPU:4 now
where the time goes in v3:
time: 77.8 us; the launch traced here: 77.6 us
  Pallas kernels  74.3 us (96%)
  local copies, waits for them, and re-layouts  2.48 us (3%)
    pallas_call x1, Pallas kernels, fetch(): pl.pallas_call(fetch_kernel, out_shape=[jax.ShapeDtypeStruct((ALL, ROWS,...  28.5 us
    pallas_call x1, Pallas kernels, send_home(): pl.pallas_call(return_kernel, out_shape=jax.ShapeDtypeStruct((PORTS, BLK...  24.8 us
    pallas_call x1, Pallas kernels, tiles(): pl.pallas_call(tiles_kernel, out_shape=jax.ShapeDtypeStruct((ALL + 1, POR...  21 us
    concatenate x1, local copies, waits for them, and re-layouts, on_device(): jnp.concatenate([positions, directions, rad, rad, currents], axis=0)  1.74 us

profile of v3, /device:TPU:4, one launch (start us, length us, event | category | flops | bytes accessed | tf_op | source)
XLA Modules:
  0.0 77.6 jit_solution(4537832305803035820)
XLA Ops:
  0.0 0.8 fusion
  0.8 0.1 reshape.8.pairs
  0.8 1.7 %concatenate.3.packed = f32[24,2048]{1,0:T(8,128)S(1)} concatenate(f32[3,2048]{1,0:T(4,128)} %param.6, f32[3,2048]{1,0:T(4,128)} %param.7, f32[1,2048]{1,0:T(1,128)} %bitcast.1, f32[1,2048]{1,0:T(1,128)} %bitcast.2, f32[16,2048]{1,0:T(8,128)} %param.9), dimensions={0} | concatenate | bytes 393216 | tf_op jit(solution)/shard_map/concatenate | solution.py:487
  2.6 28.5 %shard_map.64 = (f32[96,24,256]{2,1,0:T(8,128)S(1)}, bf16[96,96,256]{2,1,0:T(8,128)(2,1)S(1)}, f32[40,4,256,128]{3,2,1,0:T(8,128)S(1)}, f32[97,16,256]{2,1,0:T(8,128)S(1)}, s32[88,32]{1,0:T(8,128)S(1)}) custom-call(f32[24,2048]{1,0:T(8,128)S(1)} %concatenate.3.packed, s32[1,256]{1,0:T(1,128)S(1)} %reshape.8.pairs), custom_call_target="tpu_custom_call" | custom-call | tf_op jit(solution)/shard_map/pallas_call | solution.py:325
  31.1 21.0 %shard_map.65.acc = f32[97,16,256]{2,1,0:T(8,128)S(1)} custom-call(s32[88,32]{1,0:T(8,128)S(1)} %get-tuple-element.10.table, f32[96,24,256]{2,1,0:T(8,128)S(1)} %get-tuple-element.11.blocks, bf16[96,96,256]{2,1,0:T(8,128)(2,1)S(1)} %get-tuple-element.12.terms, f32[40,4,256,128]{3,2,1,0:T(8,128)S(1)} %get-tuple-element.13.cols, ...), custom_call_target="tpu_custom_call", output_to_operand_aliasing={{}: (4, {})} | custom-call | tf_op jit(solution)/shard_map/pallas_call | solution.py:391
  52.1 24.8 %shard_map.66 = f32[16,2048]{1,0:T(8,128)S(1)} custom-call(f32[97,16,256]{2,1,0:T(8,128)S(1)} %shard_map.65.acc), custom_call_target="tpu_custom_call" | custom-call | tf_op jit(solution)/shard_map/pallas_call | solution.py:465
  76.9 0.7 copy.10

commit v4 on v3

--- a/solution.py
+++ b/solution.py
@@ -41,7 +41,7 @@
     barrier = pltpu.get_barrier_semaphore()
     for device in devices:
         pl.semaphore_signal(barrier, inc=1, device_id=device, device_id_type=MESH)
-    pl.semaphore_wait(barrier, len(devices))
+    return lambda: pl.semaphore_wait(barrier, len(devices))
 
 
 def remote(src, dst, send, recv, device):
@@ -178,19 +178,34 @@
 
 
 def fetch_kernel(
-    packed, pairs,
+    pos_in, dirs_in, rad_in, cur_in, target_in, count_in,
     blocks, terms, cols, acc, table,
-    lists, tile, t_send, t_recv, y_send, y_recv, l_send, l_recv, z_send, z_recv, c_send, c_recv,
+    pos, dirs, rad, cur, target, count, in_sem, lists, tile, t_send, t_recv, y_send, y_recv, l_send, l_recv, z_send, z_recv, c_send, c_recv,
 ):
     wide, member, core, twin, ahead, behind = place()
     mates = [lax.rem(member + step, MEMBERS) for step in range(1, MEMBERS)]
+    loads = [
+        pltpu.make_async_copy(whole, held, in_sem.at[at])
+        for at, (whole, held) in enumerate(
+            [(pos_in, pos), (dirs_in, dirs), (rad_in, rad), (cur_in, cur), (target_in, target), (count_in, count)]
+        )
+    ]
+    for copy in loads:
+        copy.start()
     lists[...] = jnp.full((8, FIL), -1, jnp.int32)
-    lists[pl.ds(member, 1)] = pairs[...]
+    wait_for_greetings = greet([(wide, mate) for mate in mates] + [(ahead, member), (twin, member)])
+    for copy in loads:
+        copy.wait()
+    slot = lax.broadcasted_iota(jnp.int32, (1, MAXP), 1)
+    lists[pl.ds(member, 1)] = jnp.concatenate(
+        [jnp.where(slot < count[r], target[r : r + 1], -1) for r in range(BLK)], axis=1
+    )
     for b in range(BLK):
-        block = packed[:, b * FIL : (b + 1) * FIL]
+        cut = slice(b * FIL, (b + 1) * FIL)
+        block = jnp.concatenate([pos[:, cut], dirs[:, cut], rad[:, cut], rad[:, cut], cur[:, cut]], axis=0)
         blocks[member * BLK + b] = block
         blocks[SLAB + core * BLK + b] = block
-    greet([(wide, mate) for mate in mates] + [(ahead, member), (twin, member)])
+    wait_for_greetings()
     half = BLK // PARTS
     own = blocks.at[pl.ds(member * BLK, BLK)]
 
@@ -319,7 +334,8 @@
         copy.wait_send()
 
 
-def fetch(packed, pairs):
+def fetch(*inputs):
+    hbm = pl.BlockSpec(memory_space=pltpu.HBM)
     vm = pl.BlockSpec(memory_space=pltpu.VMEM)
     dma = pltpu.SemaphoreType.DMA
     return pl.pallas_call(
@@ -331,9 +347,16 @@
             jax.ShapeDtypeStruct((ALL + 1, PORTS, FIL), f32),
             jax.ShapeDtypeStruct((88, 32), jnp.int32),
         ],
-        in_specs=[vm] * 2,
+        in_specs=[hbm] * 6,
         out_specs=[vm] * 5,
         scratch_shapes=[
+            pltpu.VMEM((3, BLK * FIL), f32),
+            pltpu.VMEM((3, BLK * FIL), f32),
+            pltpu.VMEM((1, BLK * FIL), f32),
+            pltpu.VMEM((PORTS, BLK * FIL), f32),
+            pltpu.VMEM((BLK, MAXP), jnp.int32),
+            pltpu.SMEM((BLK,), jnp.int32),
+            dma((6,)),
             pltpu.VMEM((8, FIL), jnp.int32),
             pltpu.VMEM((FIL, FIL), bf16),
             dma, dma,
@@ -344,7 +367,7 @@
         compiler_params=pltpu.CompilerParams(
             collective_id=0, has_side_effects=True, vmem_limit_bytes=8 * 2**20
         ),
-    )(packed, pairs)
+    )(*inputs)
 
 
 def tiles_kernel(table, blocks, terms, cols, start, acc, even, odd, turns, sem):
@@ -409,7 +432,16 @@
 ):
     wide, member, core, twin, ahead, behind = place()
     mates = [lax.rem(member + step, MEMBERS) for step in range(1, MEMBERS)]
-    greet([(wide, mate) for mate in mates] + [(behind, member), (twin, member)])
+    first, last = wide < 2, wide >= lax.axis_size("wide") - 2
+    barrier = pltpu.get_barrier_semaphore()
+    for device in [(wide, mate) for mate in mates] + [(twin, member)]:
+        pl.semaphore_signal(barrier, inc=1, device_id=device, device_id_type=MESH)
+
+    @pl.when(~first)
+    def _():
+        pl.semaphore_signal(barrier, inc=1, device_id=(behind, member), device_id_type=MESH)
+
+    pl.semaphore_wait(barrier, jnp.where(last, MEMBERS, MEMBERS + 1))
     half = BLK // PARTS
     core_copies = {}
     for hop in range(HOPS - 1, -1, -1):
@@ -435,16 +467,22 @@
             core_copies[hop, part].wait_recv()
             value = x_buf[hop, cut] + acc[pl.ds(SLAB + (2 * hop + core) * BLK + part * half, half)]
             if hop < HOPS - 1:
-                hops[hop + 1, part].wait_recv()
-                value = value + z_buf[hop, cut]
+                @pl.when(~first)
+                def _():
+                    hops[hop + 1, part].wait_recv()
+
+                value = value + jnp.where(first, 0.0, z_buf[hop, cut])
             if hop > 0:
                 z_out[hop - 1, cut] = value
                 copy = remote(
                     z_out.at[hop - 1, cut], z_buf.at[hop - 1, cut],
                     z_send.at[hop - 1, part], z_recv.at[hop - 1, part], (ahead, member),
                 )
-                copy.start()
                 hops[hop, part] = copy
+
+                @pl.when(~last)
+                def _():
+                    copy.start()
             else:
                 if part == 0:
                     for copy in unit_copies:
@@ -455,8 +493,13 @@
                 for b in range(half):
                     at = (part * half + b) * FIL
                     out[:, at : at + FIL] = value[b]
-    for copy in list(core_copies.values()) + unit_copies + list(hops.values()):
+    for copy in list(core_copies.values()) + unit_copies:
         copy.wait_send()
+
+    @pl.when(~last)
+    def _():
+        for copy in hops.values():
+            copy.wait_send()
 
 
 def send_home(acc):
@@ -484,10 +527,9 @@
 
 def on_device(positions, directions, radius, currents, pair_target, pair_count):
     rad = radius.reshape(1, BLK * FIL)
-    packed = jnp.concatenate([positions, directions, rad, rad, currents], axis=0)
-    slots = jnp.arange(MAXP, dtype=jnp.int32)
-    pairs = jnp.where(slots[None, :] < pair_count[:, None], pair_target, -1).reshape(1, BLK * MAXP)
-    blocks, terms, cols, acc, table = fetch(packed, pairs)
+    inputs = (positions, directions, rad, currents, pair_target, pair_count)
+    inputs = [pltpu.with_memory_space_constraint(x, pltpu.HBM) for x in inputs]
+    blocks, terms, cols, acc, table = fetch(*inputs)
     return send_home(tiles(table, blocks, terms, cols, acc))
 
 

time: 77.8 us -> 76.7 us (0.986)
  local copies, waits for them, and re-layouts: 2.48 us -> 0.66 us
  Pallas kernels: 74.3 us -> 75.9 us
    concatenate x1 -> x0, local copies, waits for them, and re-layouts: 1.74 us -> none  [on_device(): jnp.concatenate([positions, directions, rad, rad, currents], axis=0)]
    pallas_call x1, Pallas kernels: 21 us -> 22.6 us  [tiles(): pl.pallas_call(tiles_kernel, out_shape=jax.ShapeDtypeStruct((ALL + 1, POR...]
where the time goes in v4:
time: 76.7 us; the launch traced here: 76.5 us
  Pallas kernels  75.9 us (99%)
    pallas_call x1, Pallas kernels, fetch(): pl.pallas_call(fetch_kernel, out_shape=[jax.ShapeDtypeStruct((ALL, ROWS,...  28.6 us
    pallas_call x1, Pallas kernels, send_home(): pl.pallas_call(return_kernel, out_shape=jax.ShapeDtypeStruct((PORTS, BLK...  24.7 us
    pallas_call x1, Pallas kernels, tiles(): pl.pallas_call(tiles_kernel, out_shape=jax.ShapeDtypeStruct((ALL + 1, POR...  22.6 us

profile of v4, /device:TPU:4, one launch (start us, length us, event | category | flops | bytes accessed | tf_op | source)
XLA Modules:
  0.0 76.5 jit_solution(2638820574252019599)
XLA Ops:
  0.0 28.6 %shard_map.64 = (f32[96,24,256]{2,1,0:T(8,128)S(1)}, bf16[96,96,256]{2,1,0:T(8,128)(2,1)S(1)}, f32[40,4,256,128]{3,2,1,0:T(8,128)S(1)}, f32[97,16,256]{2,1,0:T(8,128)S(1)}, s32[88,32]{1,0:T(8,128)S(1)}) custom-call(f32[3,2048]{1,0:T(4,128)} %pos_in.1, f32[3,2048]{1,0:T(4,128)} %dirs_in.1, f32[1,2048]{1,0:T(1,128)} %bitcast.1, f32[16,2048]{1,0:T(8,128)} %cur_in.1, ...), custom_call_target="tpu_custom_call" | custom-call | tf_op jit(solution)/shard_map/pallas_call | solution.py:341
  28.6 22.6 %shard_map.65.acc = f32[97,16,256]{2,1,0:T(8,128)S(1)} custom-call(s32[88,32]{1,0:T(8,128)S(1)} %get-tuple-element.10.table, f32[96,24,256]{2,1,0:T(8,128)S(1)} %get-tuple-element.11.blocks, bf16[96,96,256]{2,1,0:T(8,128)(2,1)S(1)} %get-tuple-element.12.terms, f32[40,4,256,128]{3,2,1,0:T(8,128)S(1)} %get-tuple-element.13.cols, ...), custom_call_target="tpu_custom_call", output_to_operand_aliasing={{}: (4, {})} | custom-call | tf_op jit(solution)/shard_map/pallas_call | solution.py:414
  51.2 24.7 %shard_map.66 = f32[16,2048]{1,0:T(8,128)S(1)} custom-call(f32[97,16,256]{2,1,0:T(8,128)S(1)} %shard_map.65.acc), custom_call_target="tpu_custom_call" | custom-call | tf_op jit(solution)/shard_map/pallas_call | solution.py:508
  75.9 0.7 copy.10

commit v5 on v4

--- a/solution.py
+++ b/solution.py
@@ -145,8 +145,13 @@
     return jnp.concatenate([head, tail], axis=0)
 
 
-def columns(block, spread):
-    geometry = jnp.concatenate([block[0:3], block[6:7] * block[6:7]], axis=0)
+def depth_base(wide):
+    return (wide // 2).astype(f32) * 0.2 + 0.5
+
+
+def columns(block, spread, base):
+    depth = block[2:3] - base
+    geometry = jnp.concatenate([block[0:2], -2.0 * depth, block[6:7] * block[6:7] + depth * depth], axis=0)
     head = geometry.astype(bf16).astype(f32)
     rest = geometry - head
     middle = rest.astype(bf16).astype(f32)
@@ -155,16 +160,16 @@
     return jnp.dot(terms.T.astype(bf16), spread, preferred_element_type=f32)
 
 
-def tile_pieces(cols, i, geometry, buf):
-    radius = geometry[6:7] * geometry[6:7]
+def tile_pieces(cols, i, geometry, base, buf):
+    depth = geometry[2:3] - base
+    sized = geometry[6:7] * geometry[6:7] + depth * depth
 
     def piece(h, r):
         cut = slice(h * 128, h * 128 + 128)
-        xb, yb, zb = [jnp.broadcast_to(geometry[q : q + 1, cut], (16, 128)) for q in range(3)]
-        rb = jnp.broadcast_to(radius[:, cut], (16, 128))
+        xb, yb, zb, rb = [jnp.broadcast_to(v[:, cut], (16, 128)) for v in (geometry[0:1], geometry[1:2], depth, sized)]
         xa, ya, za, ra = [cols[i, q, r : r + 16, :] for q in range(4)]
-        dx, dy, dz = xa - xb, ya - yb, za - zb
-        gap = (ra + rb) + dx * dx + dy * dy + dz * dz
+        dx, dy = xa - xb, ya - yb
+        gap = ((ra + rb) + za * zb) + dx * dx + dy * dy
         buf[r : r + 16, cut] = lax.rsqrt(gap).astype(bf16)
 
     return [functools.partial(piece, h, r) for h in range(2) for r in range(0, FIL, 16)]
@@ -236,6 +241,7 @@
     copy.start()
     core_copies[0, 0] = copy
 
+    base = depth_base(wide)
     term = lax.broadcasted_iota(jnp.int32, (16, 512), 0)
     group = lax.broadcasted_iota(jnp.int32, (16, 512), 1) // 128
     spread = jnp.where((term < 12) & (lax.rem(term, 4) == group), 1.0, 0.0).astype(bf16)
@@ -247,7 +253,7 @@
                 i = first + 4 * quad + b
                 block = blocks[i]
                 terms[i] = directed(block)
-                wide_columns = columns(block, spread)
+                wide_columns = columns(block, spread, base)
                 for q in range(4):
                     cols[held + 4 * quad + b, q] = wide_columns[:, q * 128 : (q + 1) * 128]
 
@@ -311,7 +317,7 @@
     @pl.loop(0, BLK)
     def _(b):
         i = member * BLK + b
-        for piece in tile_pieces(cols, i, blocks[i, 0:8, :], tile):
+        for piece in tile_pieces(cols, i, blocks[i, 0:8, :], base, tile):
             piece()
         product = lax.dot_general(terms[i], tile[...], (((1,), (1,)), ((), ())), preferred_element_type=f32)
         acc[i] = fold(product, blocks[i, 3:6, :])
@@ -375,6 +381,7 @@
     load.start()
     load.wait()
     n = turns[2 * LIST, 0]
+    base = depth_base(lax.axis_index("wide"))
 
     def pair(k):
         row, col = k // 32, k & 31
@@ -383,7 +390,7 @@
     def chunks(k, buf):
         i, j = pair(k)
         held = jnp.where(i < SLAB, i, SLAB + (i & (BLK - 1)))
-        return tile_pieces(cols, held, blocks[jnp.minimum(j, ALL - 1), 0:8, :], buf)
+        return tile_pieces(cols, held, blocks[jnp.minimum(j, ALL - 1), 0:8, :], base, buf)
 
     def step(k_next, buf_next, k, buf):
         work = chunks(k_next, buf_next)
@@ -401,12 +408,22 @@
     for piece in chunks(0, even):
         piece()
 
-    @pl.loop(0, (n + UNROLL - 1) // UNROLL)
-    def _(turn):
-        k = UNROLL * turn
-        for q in range(UNROLL):
+    def steps(k, count):
+        for q in range(count):
             now, later = (even, odd) if q % 2 == 0 else (odd, even)
             step(k + q + 1, later, k + q, now)
+
+    half = UNROLL // 2
+
+    @pl.loop(0, (n + half - 1) // UNROLL)
+    def _(turn):
+        steps(UNROLL * turn, UNROLL)
+
+    left = n & (UNROLL - 1)
+
+    @pl.when((left > 0) & (left <= half))
+    def _():
+        steps(n - left, half)
 
 
 def tiles(table, blocks, terms, cols, acc):

time: 76.7 us -> 74.6 us (0.973)
  Pallas kernels: 75.9 us -> 73.8 us
    pallas_call x1, Pallas kernels: 24.7 us -> 18.2 us  [send_home(): pl.pallas_call(return_kernel, out_shape=jax.ShapeDtypeStruct((PORTS, BLK...]
    pallas_call x1, Pallas kernels: 22.6 us -> 27.1 us  [tiles(): pl.pallas_call(tiles_kernel, out_shape=jax.ShapeDtypeStruct((ALL + 1, POR...]
where the time goes in v5:
time: 74.6 us; the launch traced here: 74.4 us
  Pallas kernels  73.8 us (99%)
    pallas_call x1, Pallas kernels, fetch(): pl.pallas_call(fetch_kernel, out_shape=[jax.ShapeDtypeStruct((ALL, ROWS,...  28.5 us
    pallas_call x1, Pallas kernels, tiles(): pl.pallas_call(tiles_kernel, out_shape=jax.ShapeDtypeStruct((ALL + 1, POR...  27.1 us
    pallas_call x1, Pallas kernels, send_home(): pl.pallas_call(return_kernel, out_shape=jax.ShapeDtypeStruct((PORTS, BLK...  18.2 us

profile of v5, /device:TPU:4, one launch (start us, length us, event | category | flops | bytes accessed | tf_op | source)
XLA Modules:
  0.0 74.4 jit_solution(13807651035857997871)
XLA Ops:
  0.0 28.5 %shard_map.64 = (f32[96,24,256]{2,1,0:T(8,128)S(1)}, bf16[96,96,256]{2,1,0:T(8,128)(2,1)S(1)}, f32[40,4,256,128]{3,2,1,0:T(8,128)S(1)}, f32[97,16,256]{2,1,0:T(8,128)S(1)}, s32[88,32]{1,0:T(8,128)S(1)}) custom-call(f32[3,2048]{1,0:T(4,128)} %pos_in.1, f32[3,2048]{1,0:T(4,128)} %dirs_in.1, f32[1,2048]{1,0:T(1,128)} %bitcast.1, f32[16,2048]{1,0:T(8,128)} %cur_in.1, ...), custom_call_target="tpu_custom_call" | custom-call | tf_op jit(solution)/shard_map/pallas_call | solution.py:347
  28.5 27.1 %shard_map.65.acc = f32[97,16,256]{2,1,0:T(8,128)S(1)} custom-call(s32[88,32]{1,0:T(8,128)S(1)} %get-tuple-element.10.table, f32[96,24,256]{2,1,0:T(8,128)S(1)} %get-tuple-element.11.blocks, bf16[96,96,256]{2,1,0:T(8,128)(2,1)S(1)} %get-tuple-element.12.terms, f32[40,4,256,128]{3,2,1,0:T(8,128)S(1)} %get-tuple-element.13.cols, ...), custom_call_target="tpu_custom_call", output_to_operand_aliasing={{}: (4, {})} | custom-call | tf_op jit(solution)/shard_map/pallas_call | solution.py:431
  55.6 18.2 %shard_map.66 = f32[16,2048]{1,0:T(8,128)S(1)} custom-call(f32[97,16,256]{2,1,0:T(8,128)S(1)} %shard_map.65.acc), custom_call_target="tpu_custom_call" | custom-call | tf_op jit(solution)/shard_map/pallas_call | solution.py:525
  73.8 0.7 copy.10

commit v6 on v5

--- a/solution.py
+++ b/solution.py
@@ -164,15 +164,20 @@
     depth = geometry[2:3] - base
     sized = geometry[6:7] * geometry[6:7] + depth * depth
 
-    def piece(h, r):
-        cut = slice(h * 128, h * 128 + 128)
-        xb, yb, zb, rb = [jnp.broadcast_to(v[:, cut], (16, 128)) for v in (geometry[0:1], geometry[1:2], depth, sized)]
+    def piece(r):
         xa, ya, za, ra = [cols[i, q, r : r + 16, :] for q in range(4)]
-        dx, dy = xa - xb, ya - yb
-        gap = ((ra + rb) + za * zb) + dx * dx + dy * dy
-        buf[r : r + 16, cut] = lax.rsqrt(gap).astype(bf16)
-
-    return [functools.partial(piece, h, r) for h in range(2) for r in range(0, FIL, 16)]
+        halves = []
+        for h in range(2):
+            cut = slice(h * 128, h * 128 + 128)
+            xb, yb, zb, rb = [
+                jnp.broadcast_to(v[:, cut], (16, 128)) for v in (geometry[0:1], geometry[1:2], depth, sized)
+            ]
+            dx, dy = xa - xb, ya - yb
+            gap = ((ra + rb) + za * zb) + dx * dx + dy * dy
+            halves.append(lax.rsqrt(gap).astype(bf16))
+        buf[r : r + 16, :] = jnp.concatenate(halves, axis=1)
+
+    return [functools.partial(piece, r) for r in range(0, FIL, 16)]
 
 
 def fold(product, dirs):
@@ -397,11 +402,11 @@
         i_put, j_put = pair(k)
         i, j = jnp.minimum(i_put, ALL - 1), jnp.minimum(j_put, ALL - 1)
         behind = lax.dot_general(terms[i], buf[...], (((1,), (0,)), ((), ())), preferred_element_type=f32)
-        for piece in work[:16]:
+        for piece in work[:8]:
             piece()
         acc[j_put] += fold(behind, blocks[j, 3:6, :])
         ahead = lax.dot_general(terms[j], buf[...], (((1,), (1,)), ((), ())), preferred_element_type=f32)
-        for piece in work[16:]:
+        for piece in work[8:]:
             piece()
         acc[i_put] += fold(ahead, blocks[i, 3:6, :])
 

time: 74.6 us -> 71.7 us (0.961)
  the two profiles are of different devices: /device:TPU:4 before, /device:TPU:6 now
where the time goes in v6:
time: 71.7 us; the launch traced here: 71.3 us
  Pallas kernels  70.6 us (98%)
    pallas_call x1, Pallas kernels, fetch(): pl.pallas_call(fetch_kernel, out_shape=[jax.ShapeDtypeStruct((ALL, ROWS,...  28.5 us
    pallas_call x1, Pallas kernels, send_home(): pl.pallas_call(return_kernel, out_shape=jax.ShapeDtypeStruct((PORTS, BLK...  22.2 us
    pallas_call x1, Pallas kernels, tiles(): pl.pallas_call(tiles_kernel, out_shape=jax.ShapeDtypeStruct((ALL + 1, POR...  20 us

profile of v6, /device:TPU:6, one launch (start us, length us, event | category | flops | bytes accessed | tf_op | source)
XLA Modules:
  0.0 71.3 jit_solution(11557988000500679370)
XLA Ops:
  0.0 28.5 %shard_map.64 = (f32[96,24,256]{2,1,0:T(8,128)S(1)}, bf16[96,96,256]{2,1,0:T(8,128)(2,1)S(1)}, f32[40,4,256,128]{3,2,1,0:T(8,128)S(1)}, f32[97,16,256]{2,1,0:T(8,128)S(1)}, s32[88,32]{1,0:T(8,128)S(1)}) custom-call(f32[3,2048]{1,0:T(4,128)} %pos_in.1, f32[3,2048]{1,0:T(4,128)} %dirs_in.1, f32[1,2048]{1,0:T(1,128)} %bitcast.1, f32[16,2048]{1,0:T(8,128)} %cur_in.1, ...), custom_call_target="tpu_custom_call" | custom-call | tf_op jit(solution)/shard_map/pallas_call | solution.py:352
  28.5 20.0 %shard_map.65.acc = f32[97,16,256]{2,1,0:T(8,128)S(1)} custom-call(s32[88,32]{1,0:T(8,128)S(1)} %get-tuple-element.10.table, f32[96,24,256]{2,1,0:T(8,128)S(1)} %get-tuple-element.11.blocks, bf16[96,96,256]{2,1,0:T(8,128)(2,1)S(1)} %get-tuple-element.12.terms, f32[40,4,256,128]{3,2,1,0:T(8,128)S(1)} %get-tuple-element.13.cols, ...), custom_call_target="tpu_custom_call", output_to_operand_aliasing={{}: (4, {})} | custom-call | tf_op jit(solution)/shard_map/pallas_call | solution.py:436
  48.5 22.2 %shard_map.66 = f32[16,2048]{1,0:T(8,128)S(1)} custom-call(f32[97,16,256]{2,1,0:T(8,128)S(1)} %shard_map.65.acc), custom_call_target="tpu_custom_call" | custom-call | tf_op jit(solution)/shard_map/pallas_call | solution.py:530
  70.7 0.7 copy.10
